TPU v7x, 128 devices: a whole 4x4x4 slice. The times are simulated.
128 devices in a mesh: dp: 16 (over y, x), seq: 8 (over z, core).
Axes of the slice: x: 4, y: 4, z: 4, core: 2. Of those that a mesh axis runs over, the one named last changes fastest.
Arguments:
- inputs: bfloat16 [32, 1024, 1024], P('dp', 'seq'), may hold values from -6 to 6
- cotangent: bfloat16 [32, 1024, 1024], P('dp', 'seq'), may hold values from -8 to 8
- norm_gains: float32 [2, 1024], P(None, ('dp', 'seq')), may hold values from 0.5 to 1.5
- conv_taps: float32 [3, 1024], P(None, ('dp', 'seq')), may hold values from -3 to 3
- w_in: float32 [1024, 3072], P(('dp', 'seq')), may hold values from -0.1875 to 0.1875
- w_out: float32 [1024, 1024], P(('dp', 'seq')), may hold values from -0.1875 to 0.1875
- w_gate: float32 [1024, 4608], P(('dp', 'seq')), may hold values from -0.1875 to 0.1875
- w_up: float32 [1024, 4608], P(('dp', 'seq')), may hold values from -0.1875 to 0.1875
- w_down: float32 [4608, 1024], P(('dp', 'seq')), may hold values from -0.09375 to 0.09375
- first_gains: float32 [2, 1024], P(None, ('dp', 'seq')), may hold values from -256 to 256
- first_taps: float32 [3, 1024], P(None, ('dp', 'seq')), may hold values from -128 to 128
- first_in: float32 [1024, 3072], P(('dp', 'seq')), may hold values from -128 to 128
- first_out: float32 [1024, 1024], P(('dp', 'seq')), may hold values from -128 to 128
- first_gate: float32 [1024, 4608], P(('dp', 'seq')), may hold values from -64 to 64
- first_up: float32 [1024, 4608], P(('dp', 'seq')), may hold values from -64 to 64
- first_down: float32 [4608, 1024], P(('dp', 'seq')), may hold values from -64 to 64
- second_gains: float32 [2, 1024], P(None, ('dp', 'seq')), may hold values from 6881.28 to 27525.12
- second_taps: float32 [3, 1024], P(None, ('dp', 'seq')), may hold values from 1723.5968 to 6881.28
- second_in: float32 [1024, 3072], P(('dp', 'seq')), may hold values from 1723.5968 to 6881.28
- second_out: float32 [1024, 1024], P(('dp', 'seq')), may hold values from 1723.5968 to 6881.28
- second_gate: float32 [1024, 4608], P(('dp', 'seq')), may hold values from 432.5376 to 1723.5968
- second_up: float32 [1024, 4608], P(('dp', 'seq')), may hold values from 432.5376 to 1723.5968
- second_down: float32 [4608, 1024], P(('dp', 'seq')), may hold values from 432.5376 to 1723.5968
Outputs:
- output: bfloat16 [32, 1024, 1024], P('dp', 'seq')
- input_grad: float32 [32, 1024, 1024], P('dp', 'seq')
- new_gains: float32 [2, 1024], P(None, ('dp', 'seq'))
- new_taps: float32 [3, 1024], P(None, ('dp', 'seq'))
- new_in: float32 [1024, 3072], P(('dp', 'seq'))
- new_out: float32 [1024, 1024], P(('dp', 'seq'))
- new_gate: float32 [1024, 4608], P(('dp', 'seq'))
- new_up: float32 [1024, 4608], P(('dp', 'seq'))
- new_down: float32 [4608, 1024], P(('dp', 'seq'))
- new_first_gains: float32 [2, 1024], P(None, ('dp', 'seq'))
- new_first_taps: float32 [3, 1024], P(None, ('dp', 'seq'))
- new_first_in: float32 [1024, 3072], P(('dp', 'seq'))
- new_first_out: float32 [1024, 1024], P(('dp', 'seq'))
- new_first_gate: float32 [1024, 4608], P(('dp', 'seq'))
- new_first_up: float32 [1024, 4608], P(('dp', 'seq'))
- new_first_down: float32 [4608, 1024], P(('dp', 'seq'))
- new_second_gains: float32 [2, 1024], P(None, ('dp', 'seq'))
- new_second_taps: float32 [3, 1024], P(None, ('dp', 'seq'))
- new_second_in: float32 [1024, 3072], P(('dp', 'seq'))
- new_second_out: float32 [1024, 1024], P(('dp', 'seq'))
- new_second_gate: float32 [1024, 4608], P(('dp', 'seq'))
- new_second_up: float32 [1024, 4608], P(('dp', 'seq'))
- new_second_down: float32 [4608, 1024], P(('dp', 'seq'))
All inputs are finite; a program needn't handle non-finite values.
Results may differ from a plain program's by a relative error of at most 0.019.
Values may be sent and summed in bfloat16 or wider, within the bound.
A program may use at most 256 MiB of HBM per device.

v0:
```python
import jax
import jax.numpy as jnp
from jax import lax
from jax.sharding import PartitionSpec as P

D = 1024
STEP = 5


epsilon_norm = 1e-05
beta_one = 0.9
beta_two = 0.95
epsilon_adam = 1e-08
rate_matrix = 0.02
rate_small = 0.3
weight_decay = 0.1


def shifted(value, axis, steps):
    count = lax.axis_size(axis)
    leading, last = (max(0, -steps), min(count, count - steps))
    return lax.ppermute(value, axis, [(source, source + steps) for source in range(leading, last)])


def adamw(weight, grad, first, second, rate, decay):
    first_new = beta_one * first + (1.0 - beta_one) * grad
    second_new = beta_two * second + (1.0 - beta_two) * grad * grad
    first_hat = first_new / (1.0 - beta_one**STEP)
    second_hat = second_new / (1.0 - beta_two**STEP)
    weight_new = weight - rate * (
        first_hat / (jnp.sqrt(second_hat) + epsilon_adam) + decay * weight
    )
    return (weight_new, first_new, second_new)


def norm_back(upstream, scaled, inverse, gain):
    weighted = upstream * gain
    return inverse * (weighted - scaled * jnp.mean(weighted * scaled, axis=-1, keepdims=True))


def backward_weights(lows):
    return (
        lax.all_gather(lows[0], ("dp", "seq"), axis=0, tiled=True),
        lax.all_gather(lows[1], ("dp", "seq"), axis=0, tiled=True),
        lax.all_gather(lows[2], ("dp", "seq"), axis=0, tiled=True),
        lax.all_gather(lows[3], ("dp", "seq"), axis=0, tiled=True),
        lax.all_gather(lows[4], ("dp", "seq"), axis=0, tiled=True),
    )


def shards(
    inputs,
    cotangent,
    norm_gains,
    conv_taps,
    w_in,
    w_out,
    w_gate,
    w_up,
    w_down,
    first_gains,
    first_taps,
    first_in,
    first_out,
    first_gate,
    first_up,
    first_down,
    second_gains,
    second_taps,
    second_in,
    second_out,
    second_gate,
    second_up,
    second_down,
):
    bf16 = jnp.bfloat16
    single_float = jnp.float32
    span_rows = inputs.shape[1]
    gains_low = norm_gains.astype(bf16)
    taps_low = conv_taps.astype(bf16)
    input_weight_reduced = w_in.astype(bf16)
    output_weight_reduced = w_out.astype(bf16)
    gate_weight_reduced = w_gate.astype(bf16)
    up_weight_reduced = w_up.astype(bf16)
    down_weight_reduced = w_down.astype(bf16)
    gains_full, taps_full, input_weight_float, output_weight_float = (
        lax.all_gather(gains_low, ("dp", "seq"), axis=1, tiled=True),
        lax.all_gather(taps_low, ("dp", "seq"), axis=1, tiled=True),
        lax.all_gather(input_weight_reduced, ("dp", "seq"), axis=0, tiled=True),
        lax.all_gather(output_weight_reduced, ("dp", "seq"), axis=0, tiled=True),
    )
    gate_weight_float, up_weight_float, down_weight_float = (
        lax.all_gather(gate_weight_reduced, ("dp", "seq"), axis=0, tiled=True),
        lax.all_gather(up_weight_reduced, ("dp", "seq"), axis=0, tiled=True),
        lax.all_gather(down_weight_reduced, ("dp", "seq"), axis=0, tiled=True),
    )
    gains_wide = gains_full.astype(single_float)
    taps_wide = taps_full.astype(single_float)
    lows = (
        input_weight_reduced,
        output_weight_reduced,
        gate_weight_reduced,
        up_weight_reduced,
        down_weight_reduced,
    )
    widened_inputs = inputs.astype(single_float)
    inverse = lax.rsqrt(
        jnp.mean(widened_inputs * widened_inputs, axis=-1, keepdims=True) + epsilon_norm
    )
    scaled = widened_inputs * inverse
    normalized_input = (scaled * gains_wide[0]).astype(bf16)
    grad_wide = cotangent.astype(single_float)
    narrow_hidden_gradient = grad_wide.astype(bf16)
    projected_rows = jnp.einsum(
        "hyf,fi->hyi", normalized_input, input_weight_float, preferred_element_type=single_float
    )
    b_part = projected_rows[..., :D]
    c_part = projected_rows[..., D : 2 * D]
    x_part = projected_rows[..., 2 * D :]
    gated = b_part * x_part
    earlier = shifted(gated[:, span_rows - 2 :, :], "seq", 1)
    extended = jnp.concatenate([earlier, gated], axis=1)
    convolved = (
        taps_wide[0] * extended[:, :-2]
        + taps_wide[1] * extended[:, 1:-1]
        + taps_wide[2] * extended[:, 2:]
    )
    mixer_input_rows = (c_part * convolved).astype(bf16)
    hidden_state = widened_inputs + jnp.einsum(
        "hyf,fi->hyi", mixer_input_rows, output_weight_float, preferred_element_type=single_float
    )
    inverse_two = lax.rsqrt(
        jnp.mean(hidden_state * hidden_state, axis=-1, keepdims=True) + epsilon_norm
    )
    scaled_two = hidden_state * inverse_two
    normalized_second = (scaled_two * gains_wide[1]).astype(bf16)
    gate_projection_value = jnp.einsum(
        "wzj,jg->wzg", normalized_second, gate_weight_float, preferred_element_type=single_float
    )
    up_projection_value = jnp.einsum(
        "wzj,jg->wzg", normalized_second, up_weight_float, preferred_element_type=single_float
    )
    activated_hidden = (jax.nn.silu(gate_projection_value) * up_projection_value).astype(bf16)
    output = (
        hidden_state
        + jnp.einsum(
            "omb,bu->omu", activated_hidden, down_weight_float, preferred_element_type=single_float
        )
    ).astype(bf16)
    (
        input_weight_return,
        output_weight_return,
        gate_weight_return,
        up_weight_return,
        down_weight_return,
    ) = backward_weights(lows)
    down_weight_gradient = jnp.einsum(
        "wvj,wva->ja", activated_hidden, narrow_hidden_gradient, preferred_element_type=single_float
    )
    activated_gradient = jnp.einsum(
        "waj,hj->wah",
        narrow_hidden_gradient,
        down_weight_return,
        preferred_element_type=single_float,
    )
    sigmoid_gate = jax.nn.sigmoid(gate_projection_value)
    up_projection_gradient = (activated_gradient * (gate_projection_value * sigmoid_gate)).astype(
        bf16
    )
    gate_projection_gradient = (
        activated_gradient
        * up_projection_value
        * (sigmoid_gate * (1.0 + gate_projection_value * (1.0 - sigmoid_gate)))
    ).astype(bf16)
    gate_weight_gradient = jnp.einsum(
        "rch,rck->hk",
        normalized_second,
        gate_projection_gradient,
        preferred_element_type=single_float,
    )
    up_weight_gradient = jnp.einsum(
        "rch,rck->hk",
        normalized_second,
        up_projection_gradient,
        preferred_element_type=single_float,
    )
    grad_normed_two = jnp.einsum(
        "nbz,xz->nbx",
        gate_projection_gradient,
        gate_weight_return,
        preferred_element_type=single_float,
    ) + jnp.einsum(
        "nbz,xz->nbx", up_projection_gradient, up_weight_return, preferred_element_type=single_float
    )
    grad_gain_two = jnp.sum(grad_normed_two * scaled_two, axis=(0, 1))
    grad_hidden = grad_wide + norm_back(grad_normed_two, scaled_two, inverse_two, gains_wide[1])
    red_gate, red_up, red_down = (
        lax.psum_scatter(gate_weight_gradient, ("dp", "seq"), scatter_dimension=0, tiled=True),
        lax.psum_scatter(up_weight_gradient, ("dp", "seq"), scatter_dimension=0, tiled=True),
        lax.psum_scatter(down_weight_gradient, ("dp", "seq"), scatter_dimension=0, tiled=True),
    )
    narrow_hidden_state = grad_hidden.astype(bf16)
    output_weight_gradient = jnp.einsum(
        "yqm,yqc->mc", mixer_input_rows, narrow_hidden_state, preferred_element_type=single_float
    )
    mixer_input_gradient = jnp.einsum(
        "uby,ry->ubr",
        narrow_hidden_state,
        output_weight_return,
        preferred_element_type=single_float,
    )
    grad_c = mixer_input_gradient * convolved
    grad_conv = mixer_input_gradient * c_part
    grad_taps = jnp.stack(
        [
            jnp.sum(grad_conv * extended[:, 0:span_rows], axis=(0, 1)),
            jnp.sum(grad_conv * extended[:, 1 : span_rows + 1], axis=(0, 1)),
            jnp.sum(grad_conv * extended[:, 2:], axis=(0, 1)),
        ]
    )
    padded_grad = jnp.pad(grad_conv, ((0, 0), (2, 2), (0, 0)))
    grad_extended = (
        taps_wide[0] * padded_grad[:, 2:]
        + taps_wide[1] * padded_grad[:, 1:-1]
        + taps_wide[2] * padded_grad[:, :-2]
    )
    returned = shifted(grad_extended[:, :2, :], "seq", -1)
    grad_gated = grad_extended[:, 2:] + jnp.pad(returned, ((0, 0), (span_rows - 2, 0), (0, 0)))
    projected_gradient = jnp.concatenate(
        [grad_gated * x_part, grad_c, grad_gated * b_part], axis=-1
    ).astype(bf16)
    input_weight_gradient = jnp.einsum(
        "yqm,yqc->mc", normalized_input, projected_gradient, preferred_element_type=single_float
    )
    normalized_gradient = jnp.einsum(
        "uby,ry->ubr", projected_gradient, input_weight_return, preferred_element_type=single_float
    )
    grad_gain_one = jnp.sum(normalized_gradient * scaled, axis=(0, 1))
    input_grad = grad_hidden + norm_back(normalized_gradient, scaled, inverse, gains_wide[0])
    red_gains, red_taps, red_in, red_out = (
        lax.psum_scatter(
            jnp.stack([grad_gain_one, grad_gain_two]),
            ("dp", "seq"),
            scatter_dimension=1,
            tiled=True,
        ),
        lax.psum_scatter(grad_taps, ("dp", "seq"), scatter_dimension=1, tiled=True),
        lax.psum_scatter(input_weight_gradient, ("dp", "seq"), scatter_dimension=0, tiled=True),
        lax.psum_scatter(output_weight_gradient, ("dp", "seq"), scatter_dimension=0, tiled=True),
    )
    new_gains, new_first_gains, new_second_gains = adamw(
        norm_gains, red_gains, first_gains, second_gains, rate_small, 0.0
    )
    new_taps, new_first_taps, new_second_taps = adamw(
        conv_taps, red_taps, first_taps, second_taps, rate_small, 0.0
    )
    new_in, new_first_in, new_second_in = adamw(
        w_in, red_in, first_in, second_in, rate_matrix, weight_decay
    )
    new_out, new_first_out, new_second_out = adamw(
        w_out, red_out, first_out, second_out, rate_matrix, weight_decay
    )
    new_gate, new_first_gate, new_second_gate = adamw(
        w_gate, red_gate, first_gate, second_gate, rate_matrix, weight_decay
    )
    new_up, new_first_up, new_second_up = adamw(
        w_up, red_up, first_up, second_up, rate_matrix, weight_decay
    )
    new_down, new_first_down, new_second_down = adamw(
        w_down, red_down, first_down, second_down, rate_matrix, weight_decay
    )
    return (
        output,
        input_grad,
        new_gains,
        new_taps,
        new_in,
        new_out,
        new_gate,
        new_up,
        new_down,
        new_first_gains,
        new_first_taps,
        new_first_in,
        new_first_out,
        new_first_gate,
        new_first_up,
        new_first_down,
        new_second_gains,
        new_second_taps,
        new_second_in,
        new_second_out,
        new_second_gate,
        new_second_up,
        new_second_down,
    )


def solution(mesh):
    in_specs = (
        P("dp", "seq", None),
        P("dp", "seq", None),
        P(None, ("dp", "seq")),
        P(None, ("dp", "seq")),
        P(("dp", "seq"), None),
        P(("dp", "seq"), None),
        P(("dp", "seq"), None),
        P(("dp", "seq"), None),
        P(("dp", "seq"), None),
        P(None, ("dp", "seq")),
        P(None, ("dp", "seq")),
        P(("dp", "seq"), None),
        P(("dp", "seq"), None),
        P(("dp", "seq"), None),
        P(("dp", "seq"), None),
        P(("dp", "seq"), None),
        P(None, ("dp", "seq")),
        P(None, ("dp", "seq")),
        P(("dp", "seq"), None),
        P(("dp", "seq"), None),
        P(("dp", "seq"), None),
        P(("dp", "seq"), None),
        P(("dp", "seq"), None),
    )
    out_specs = (
        P("dp", "seq", None),
        P("dp", "seq", None),
        P(None, ("dp", "seq")),
        P(None, ("dp", "seq")),
        P(("dp", "seq"), None),
        P(("dp", "seq"), None),
        P(("dp", "seq"), None),
        P(("dp", "seq"), None),
        P(("dp", "seq"), None),
        P(None, ("dp", "seq")),
        P(None, ("dp", "seq")),
        P(("dp", "seq"), None),
        P(("dp", "seq"), None),
        P(("dp", "seq"), None),
        P(("dp", "seq"), None),
        P(("dp", "seq"), None),
        P(None, ("dp", "seq")),
        P(None, ("dp", "seq")),
        P(("dp", "seq"), None),
        P(("dp", "seq"), None),
        P(("dp", "seq"), None),
        P(("dp", "seq"), None),
        P(("dp", "seq"), None),
    )
    return jax.shard_map(shards, mesh=mesh, in_specs=in_specs, out_specs=out_specs, check_vma=False)
```

profile of v0, /device:TPU:1, one launch (start us, length us, event | category | flops | bytes accessed | tf_op | source)
XLA Modules:
  0.0 1740.1 jit_solution(13054139059855010215)
XLA Ops:
  7.2 1.5 convert_element_type.67
  8.8 1.4 convert_element_type.71
  10.3 1.6 convert_bitcast_fusion
  11.9 1.6 convert_element_type.74
  13.5 1.6 convert_element_type.73
  15.2 0.7 convert_bitcast_fusion.2
  15.9 34.4 %all-gather = bf16[128,8,2]{1,2,0:T(2,128)(2,1)S(1)} all-gather(bf16[1,8,2]{1,2,0:T(2,128)(2,1)S(1)} %convert_bitcast_fusion.2), channel_id=1, replica_groups=mesh['dp'=16,'seq'=8] {'dp','seq'}, dimensions={0}, use_global_device_ids=true | all-gather | bytes 4128 | tf_op jit(solution)/shard_map/all_gather | solution.py:87
  50.5 0.7 convert_bitcast_fusion.1
  51.2 32.9 %all-gather.1 = bf16[128,8,3]{1,2,0:T(4,128)(2,1)S(1)} all-gather(bf16[1,8,3]{1,2,0:T(4,128)(2,1)S(1)} %convert_bitcast_fusion.1), channel_id=1, replica_groups=mesh['dp'=16,'seq'=8] {'dp','seq'}, dimensions={0}, use_global_device_ids=true | all-gather | bytes 6192 | tf_op jit(solution)/shard_map/all_gather | solution.py:88
  84.5 1.2 fusion.35
  85.8 4.8 fusion.11
  90.8 2.8 collective-permute-start
  94.3 1.3 multiply_convert_fusion.7
  95.6 54.8 %all-gather.11.cloned.1.call-done = bf16[1024,1024]{1,0:T(8,128)(2,1)} async-done(((bf16[8,1024]{1,0:T(8,128)(2,1)}), bf16[1024,1024]{1,0:T(8,128)(2,1)}) %all-gather.11.cloned.1.call-update) | async-done | bytes 2097168 | tf_op jit(solution)/shard_map/all_gather | solution.py:90
  150.4 2.4 multiply_reduce_fusion.5
  153.0 70.2 %all-gather.17.cloned.1.call-done = bf16[128,36,1024]{2,1,0:T(8,128)(2,1)} async-done(((bf16[1,36,1024]{2,1,0:T(8,128)(2,1)}), bf16[128,36,1024]{2,1,0:T(8,128)(2,1)}) %all-gather.17.cloned.1.call-update) | async-done | bytes 9437200 | tf_op jit(solution)/shard_map/all_gather | solution.py:95
  223.2 13.2 reshape.87
  236.3 8.7 fusion.58
  245.0 50.7 %all-gather.15.cloned.1.call-done = bf16[1024,4608]{1,0:T(8,128)(2,1)} async-done(((bf16[8,4608]{1,0:T(8,128)(2,1)}), bf16[1024,4608]{1,0:T(8,128)(2,1)}) %all-gather.15.cloned.1.call-update) | async-done | bytes 9437200 | tf_op jit(solution)/shard_map/all_gather | solution.py:94
  295.7 7.9 fusion.3
  303.6 64.0 %all-gather.13.cloned.1.call-done = bf16[1024,4608]{1,0:T(8,128)(2,1)} async-done(((bf16[8,4608]{1,0:T(8,128)(2,1)}), bf16[1024,4608]{1,0:T(8,128)(2,1)}) %all-gather.13.cloned.1.call-update) | async-done | bytes 9437200 | tf_op jit(solution)/shard_map/all_gather | solution.py:93
  367.6 10.8 multiply_convert_fusion.1
  378.3 2.6 fusion.1
  381.0 5.5 multiply_reduce_fusion.3
  386.6 1.6 multiply_add_fusion.1
  388.2 2.8 convolution_bitcast_fusion.4
  391.3 2.5 fusion.14
  395.1 2.2 collective-permute-start.1
  397.3 2.9 collective-permute-done.1
  400.6 6.4 convolution_bitcast_fusion.3
  407.1 9.6 convolution_bitcast_fusion.2
  416.8 9.6 convolution_bitcast_fusion.1
  426.4 1.0 copy-done.7
  427.4 9.6 convolution_bitcast_fusion
  437.0 360.5 %fusion = f32[40,1024]{1,0:T(8,128)S(1)} fusion(f32[4608,1024]{1,0:T(8,128)} %convolution_bitcast_fusion), kind=kCustom, calls=%all-reduce-scatter | all-reduce-scatter fusion | flops 5242881 | bytes 19038208
  798.2 1.3 collective-permute-start.13
  799.5 2.0 collective-permute-start.12
  801.4 1.9 collective-permute-start.11
  803.4 1.9 collective-permute-start.10
  805.3 1.9 collective-permute-start.14
  807.3 7.9 fusion.27
  815.2 4.8 fusion.34
  820.2 1.3 fusion.33
  821.4 72.5 %all-reduce.6 = (f32[2,1024]{1,0:T(2,128)S(1)}, f32[3,1024]{1,0:T(4,128)S(1)}) all-reduce(f32[2,1024]{1,0:T(2,128)S(1)} %pad_maximum_fusion.5, f32[3,1024]{1,0:T(4,128)S(1)} %pad_maximum_fusion.4), channel_id=2, replica_groups=mesh['dp'=16,'seq'=8] {'dp','seq'}, use_global_device_ids=true, to_apply=%region_6.7.clone | all-reduce | flops 5120 | bytes 40960
  893.9 4.1 collective-permute-start.9
  898.0 2.6 collective-permute-start.8
  900.7 3.4 collective-permute-start.7
  904.8 1.9 collective-permute-start.6
  906.7 5.0 collective-permute-start.5
  911.7 3.8 collective-permute-start.4
  915.5 2.9 collective-permute-start.3
  918.4 2.6 collective-permute-start.2
  921.8 1.3 collective-permute-done.3
  923.8 1.1 collective-permute-done.2
  924.9 10.8 concatenate.9
  935.7 1.9 multiply_subtract_fusion
  937.6 88.1 %reduce-scatter.11.cloned.1.call-done = f32[8,1024]{1,0:T(8,128)} async-done(((f32[1024,1024]{1,0:T(8,128)}), f32[8,1024]{1,0:T(8,128)}) %reduce-scatter.11.cloned.1.call-update) | async-done | bytes 32784 | tf_op jit(solution)/shard_map/reduce_scatter | solution.py:249
  1025.7 1.4 multiply_subtract_fusion.4
  1027.1 224.7 %reduce-scatter.9.cloned.1.call-done = f32[8,3072]{1,0:T(8,128)} async-done(((f32[1024,3072]{1,0:T(8,128)}), f32[8,3072]{1,0:T(8,128)}) %reduce-scatter.9.cloned.1.call-update) | async-done | bytes 98320 | tf_op jit(solution)/shard_map/reduce_scatter | solution.py:248
  1251.9 1.7 multiply_subtract_fusion.3
  1253.6 238.7 %reduce-scatter.13.cloned.1.call-done = f32[8,4608]{1,0:T(8,128)} async-done(((f32[1024,4608]{1,0:T(8,128)}), f32[8,4608]{1,0:T(8,128)}) %reduce-scatter.13.cloned.1.call-update) | async-done | bytes 147472 | tf_op jit(solution)/shard_map/reduce_scatter | solution.py:198
  1492.3 1.9 multiply_subtract_fusion.2
  1494.2 237.6 %reduce-scatter.15.cloned.1.call-done = f32[8,4608]{1,0:T(8,128)} async-done(((f32[1024,4608]{1,0:T(8,128)}), f32[8,4608]{1,0:T(8,128)}) %reduce-scatter.15.cloned.1.call-update) | async-done | bytes 147472 | tf_op jit(solution)/shard_map/reduce_scatter | solution.py:199
  1731.8 1.7 multiply_subtract_fusion.1
  (128 shorter events, 7.0 us)
Async XLA Ops:
  7.2 78.6 %all-gather.9.cloned.1.call-start = ((), (), s32[]{:S(2)}) async-start(), calls=%async_computation.4 | async-start | bytes 6340608 | tf_op jit(solution)/shard_map/all_gather | solution.py:89
  8.8 141.6 %all-gather.11.cloned.1.call-start = ((), (), s32[]{:S(2)}) async-start(), calls=%async_computation.5 | async-start | bytes 2113536 | tf_op jit(solution)/shard_map/all_gather | solution.py:90
  10.2 213.0 %all-gather.17.cloned.1.call-start = ((), (), s32[]{:S(2)}) async-start(), calls=%async_computation.12 | async-start | bytes 10567680 | tf_op jit(solution)/shard_map/all_gather | solution.py:95
  11.9 283.8 %all-gather.15.cloned.1.call-start = ((), (), s32[]{:S(2)}) async-start(), calls=%async_computation.7 | async-start | bytes 9510912 | tf_op jit(solution)/shard_map/all_gather | solution.py:94
  13.5 354.1 %all-gather.13.cloned.1.call-start = ((), (), s32[]{:S(2)}) async-start(), calls=%async_computation.6 | async-start | bytes 9510912 | tf_op jit(solution)/shard_map/all_gather | solution.py:93
  15.1 1010.6 %reduce-scatter.11.cloned.1.call-start = ((), (), s32[]{:S(2)}) async-start(), calls=%async_computation.9 | async-start | bytes 4227072 | tf_op jit(solution)/shard_map/reduce_scatter | solution.py:249
  90.6 3.6 copy-start
  90.6 59.8 %copy-start.5 = (bf16[2,128,1024]{2,1,0:T(8,128)(2,1)S(1)}, bf16[2,128,1024]{2,1,0:T(8,128)(2,1)}, u32[]{:S(2)}) copy-start(bf16[2,128,1024]{2,1,0:T(8,128)(2,1)} %param.23) | copy-start | bytes 1572868
  90.8 3.4 collective-permute-start
  95.6 57.2 %copy-start.8 = (bf16[2,128,1024]{2,1,0:T(8,128)(2,1)}, bf16[2,128,1024]{2,1,0:T(8,128)(2,1)S(1)}, u32[]{:S(2)}) copy-start(bf16[2,128,1024]{2,1,0:T(8,128)(2,1)S(1)} %get-tuple-element.54) | copy-start | bytes 1572868
  152.8 228.2 %copy-start.3 = (f32[2,128,1024]{2,1,0:T(8,128)}, f32[2,128,1024]{2,1,0:T(8,128)S(1)}, u32[]{:S(2)}) copy-start(f32[2,128,1024]{2,1,0:T(8,128)S(1)} %get-tuple-element.68) | copy-start | bytes 3145732
  367.6 10.8 copy-start.2
  378.3 2.6 copy-start.11
  378.3 2.7 copy-start.12
  381.0 5.6 copy-start.6
  386.5 1.6 copy-start.9
  391.1 860.8 %reduce-scatter.9.cloned.1.call-start = ((), (), s32[]{:S(2)}) async-start(), calls=%async_computation.8 | async-start | bytes 12681216 | tf_op jit(solution)/shard_map/reduce_scatter | solution.py:248
  391.3 2.5 copy-start.1
  391.3 2.8 copy-start.10
  394.8 5.8 copy-start.13
  395.1 5.1 collective-permute-start.1
  400.6 6.5 copy-start.15
  400.6 6.5 copy-start.17
  407.1 1085.3 %reduce-scatter.13.cloned.1.call-start = ((), (), s32[]{:S(2)}) async-start(), calls=%async_computation.10 | async-start | bytes 19021824 | tf_op jit(solution)/shard_map/reduce_scatter | solution.py:198
  416.7 1315.1 %reduce-scatter.15.cloned.1.call-start = ((), (), s32[]{:S(2)}) async-start(), calls=%async_computation.11 | async-start | bytes 19021824 | tf_op jit(solution)/shard_map/reduce_scatter | solution.py:199
  426.4 1.0 copy-start.7
  437.0 370.3 %copy-start.4 = (f32[2,128,1024]{2,1,0:T(8,128)S(1)}, f32[2,128,1024]{2,1,0:T(8,128)}, u32[]{:S(2)}) copy-start(f32[2,128,1024]{2,1,0:T(8,128)} %copy-done.3) | copy-start | bytes 3145732
  798.2 99.8 %collective-permute-start.13 = (f32[40,1024]{1,0:T(8,128)S(1)}, f32[40,1024]{1,0:T(8,128)S(1)}, u32[]{:S(2)}, u32[]{:S(2)}) collective-permute-start(f32[40,1024]{1,0:T(8,128)S(1)} %fusion), channel_id=1, source_target_pairs={{0,12},{1,13},{2,14},{3,15},{4,16},{5,17},{6,18},{7,19},{8,20},{9,... | collective-permute-start | bytes 491528
  799.5 101.2 %collective-permute-start.12 = (f32[40,1024]{1,0:T(8,128)S(1)}, f32[40,1024]{1,0:T(8,128)}, u32[]{:S(2)}, u32[]{:S(2)}) collective-permute-start(f32[40,1024]{1,0:T(8,128)S(1)} %fusion), channel_id=1, source_target_pairs={{0,11},{1,12},{2,13},{3,14},{4,15},{5,16},{6,17},{7,18},{8,19},{9,... | collective-permute-start | bytes 491528
  801.4 103.4 %collective-permute-start.11 = (f32[40,1024]{1,0:T(8,128)S(1)}, f32[40,1024]{1,0:T(8,128)}, u32[]{:S(2)}, u32[]{:S(2)}) collective-permute-start(f32[40,1024]{1,0:T(8,128)S(1)} %fusion), channel_id=1, source_target_pairs={{0,10},{1,11},{2,12},{3,13},{4,14},{5,15},{6,16},{7,17},{8,18},{9,... | collective-permute-start | bytes 491528
  803.4 103.3 %collective-permute-start.10 = (f32[40,1024]{1,0:T(8,128)S(1)}, f32[40,1024]{1,0:T(8,128)}, u32[]{:S(2)}, u32[]{:S(2)}) collective-permute-start(f32[40,1024]{1,0:T(8,128)S(1)} %fusion), channel_id=1, source_target_pairs={{0,9},{1,10},{2,11},{3,12},{4,13},{5,14},{6,15},{7,16},{8,17},{9,1... | collective-permute-start | bytes 491528
  805.3 88.6 %collective-permute-start.14 = (f32[28,1024]{1,0:T(8,128)}, f32[28,1024]{1,0:T(8,128)}, u32[]{:S(2)}, u32[]{:S(2)}) collective-permute-start(f32[28,1024]{1,0:T(8,128)} %slice.84), channel_id=1, source_target_pairs={{0,13},{1,14},{2,15},{3,16},{4,17},{5,18},{6,19},{7,20},{8,21},{9,... | collective-permute-start | bytes 344072
  807.3 7.9 copy-start.14
  807.3 7.9 copy-start.16
  807.3 7.9 copy-start.18
  820.1 84.0 %copy-start.31 = (f32[3,8]{1,0:T(4,128)S(1)}, f32[3,8]{1,0:T(4,128)}, u32[]{:S(2)}) copy-start(f32[3,8]{1,0:T(4,128)} %param.26) | copy-start | bytes 292
  820.1 84.0 %copy-start.32 = (f32[3,8]{1,0:T(4,128)S(1)}, f32[3,8]{1,0:T(4,128)}, u32[]{:S(2)}) copy-start(f32[3,8]{1,0:T(4,128)} %param.33) | copy-start | bytes 292
  820.1 84.0 %copy-start.33 = (f32[3,8]{1,0:T(4,128)S(1)}, f32[3,8]{1,0:T(4,128)}, u32[]{:S(2)}) copy-start(f32[3,8]{1,0:T(4,128)} %param.40) | copy-start | bytes 292
  820.1 101.0 %copy-start.34 = (f32[2,8]{1,0:T(2,128)S(1)}, f32[2,8]{1,0:T(2,128)}, u32[]{:S(2)}) copy-start(f32[2,8]{1,0:T(2,128)} %param.25) | copy-start | bytes 196
  820.1 101.0 %copy-start.35 = (f32[2,8]{1,0:T(2,128)S(1)}, f32[2,8]{1,0:T(2,128)}, u32[]{:S(2)}) copy-start(f32[2,8]{1,0:T(2,128)} %param.32) | copy-start | bytes 196
  820.1 100.9 %copy-start.36 = (f32[2,8]{1,0:T(2,128)S(1)}, f32[2,8]{1,0:T(2,128)}, u32[]{:S(2)}) copy-start(f32[2,8]{1,0:T(2,128)} %param.39) | copy-start | bytes 196
  821.4 114.3 %copy-start.19 = (f32[36,1024]{1,0:T(8,128)S(1)}, f32[36,1024]{1,0:T(8,128)}, u32[]{:S(2)}) copy-start(f32[36,1024]{1,0:T(8,128)} %param.31) | copy-start | bytes 442372
  821.4 204.3 %copy-start.30 = (f32[8,1024]{1,0:T(8,128)S(1)}, f32[8,1024]{1,0:T(8,128)}, u32[]{:S(2)}) copy-start(f32[8,1024]{1,0:T(8,128)} %param.28) | copy-start | bytes 98308
  821.4 430.4 %copy-start.22 = (f32[8,3072]{1,0:T(8,128)S(1)}, f32[8,3072]{1,0:T(8,128)}, u32[]{:S(2)}) copy-start(f32[8,3072]{1,0:T(8,128)} %param.27) | copy-start | bytes 294916
  893.9 17.8 %collective-permute-start.9 = (f32[40,1024]{1,0:T(8,128)S(1)}, f32[40,1024]{1,0:T(8,128)S(1)}, u32[]{:S(2)}, u32[]{:S(2)}) collective-permute-start(f32[40,1024]{1,0:T(8,128)S(1)} %fusion), channel_id=1, source_target_pairs={{0,8},{1,9},{2,10},{3,11},{4,12},{5,13},{6,14},{7,15},{8,16},{9,17... | collective-permute-start | bytes 491528
  898.0 17.5 %collective-permute-start.8 = (f32[40,1024]{1,0:T(8,128)S(1)}, f32[40,1024]{1,0:T(8,128)S(1)}, u32[]{:S(2)}, u32[]{:S(2)}) collective-permute-start(f32[40,1024]{1,0:T(8,128)S(1)} %fusion), channel_id=1, source_target_pairs={{0,7},{1,8},{2,9},{3,10},{4,11},{5,12},{6,13},{7,14},{8,15},{9,16}... | collective-permute-start | bytes 491528
  900.7 17.8 %collective-permute-start.7 = (f32[40,1024]{1,0:T(8,128)S(1)}, f32[40,1024]{1,0:T(8,128)S(1)}, u32[]{:S(2)}, u32[]{:S(2)}) collective-permute-start(f32[40,1024]{1,0:T(8,128)S(1)} %fusion), channel_id=1, source_target_pairs={{0,6},{1,7},{2,8},{3,9},{4,10},{5,11},{6,12},{7,13},{8,14},{9,15},... | collective-permute-start | bytes 491528
  904.8 17.0 collective-permute-start.6
  906.7 15.1 collective-permute-start.5
  911.7 10.1 collective-permute-start.4
  915.5 7.6 collective-permute-start.3
  918.4 2.6 copy-start.23
  918.4 6.5 collective-permute-start.2
  921.8 570.6 %copy-start.20 = (f32[8,4608]{1,0:T(8,128)S(1)}, f32[8,4608]{1,0:T(8,128)}, u32[]{:S(2)}) copy-start(f32[8,4608]{1,0:T(8,128)} %param.29) | copy-start | bytes 442372
  921.8 810.1 %copy-start.21 = (f32[8,4608]{1,0:T(8,128)S(1)}, f32[8,4608]{1,0:T(8,128)}, u32[]{:S(2)}) copy-start(f32[8,4608]{1,0:T(8,128)} %param.30) | copy-start | bytes 442372
  921.8 1.3 copy-start.24
  921.8 1.3 copy-start.25
  921.8 1.3 copy-start.26
  923.1 0.7 copy-start.27
  935.7 796.2 %copy-start.28 = (f32[8,4608]{1,0:T(8,128)S(1)}, f32[8,4608]{1,0:T(8,128)}, u32[]{:S(2)}) copy-start(f32[8,4608]{1,0:T(8,128)} %param.37) | copy-start | bytes 442372
  935.7 796.1 %copy-start.29 = (f32[8,4608]{1,0:T(8,128)S(1)}, f32[8,4608]{1,0:T(8,128)}, u32[]{:S(2)}) copy-start(f32[8,4608]{1,0:T(8,128)} %param.44) | copy-start | bytes 442372
Sparse Core Ops, SparseCore 0:
  11.6 71.8 all-gather.8
  87.3 63.0 all-gather.10
  154.1 69.0 all-gather.16
  226.6 69.0 all-gather.14
  299.1 68.3 all-gather.12
  391.2 634.4 reduce-scatter.10
  1031.4 220.3 reduce-scatter.8
  1258.0 234.2 reduce-scatter.12
  1497.6 234.1 reduce-scatter.14
where the time goes:
time: 1740 us
  waiting for transfers between devices  1030 us (59%)
  blocking collectives  500 us (29%)
  matrix products  96 us (6%)
  starting transfers between devices  40.9 us (2%)
  local copies, waits for them, and re-layouts  27.4 us (2%)
  other arithmetic  26.1 us (2%)
    unnamed x2, blocking collectives  433 us
    reduce_scatter x1, waiting for transfers between devices, shards(): lax.psum_scatter(gate_weight_gradient, ('dp', 'seq'), scatter_dimension=0...  239 us
    reduce_scatter x1, waiting for transfers between devices, shards(): lax.psum_scatter(up_weight_gradient, ('dp', 'seq'), scatter_dimension=0,...  238 us
    reduce_scatter x1, waiting for transfers between devices, shards(): lax.psum_scatter(input_weight_gradient, ('dp', 'seq'), scatter_dimension=...  225 us
    reduce_scatter x1, waiting for transfers between devices, shards(): lax.psum_scatter(output_weight_gradient, ('dp', 'seq'), scatter_dimension...  88.1 us
    all_gather x1, waiting for transfers between devices, shards(): lax.all_gather(down_weight_reduced, ('dp', 'seq'), axis=0, tiled=True)  70.2 us
    all_gather x1, waiting for transfers between devices, shards(): lax.all_gather(gate_weight_reduced, ('dp', 'seq'), axis=0, tiled=True)  64 us
    all_gather x1, waiting for transfers between devices, shards(): lax.all_gather(output_weight_reduced, ('dp', 'seq'), axis=0, tiled=True)  54.8 us
  transfers between devices with their start and end apart: 24, of which 12 were waited for; matrix products, arithmetic and copies ran while one was open for 28% of the time, Pallas kernels for 0%

commit v1 on v0

v1 whole, which is shorter than its diff:
```python
import functools
import types

import jax
import jax.numpy as jnp
from jax import lax
from jax.experimental import pallas as pl
from jax.experimental.pallas import tpu as pltpu
from jax.sharding import PartitionSpec as P

D = 1024
STEP = 5

epsilon_norm = 1e-05
beta_one = 0.9
beta_two = 0.95
epsilon_adam = 1e-08
rate_matrix = 0.02
rate_small = 0.3
weight_decay = 0.1

MESH = pl.DeviceIdType.MESH
BF = jnp.bfloat16
F32 = jnp.float32
SIDE = 4
PEERS = 8
OWN = 36
PACKED = 2304
SLICE = 576
WIDE = 512
VMEM_BYTES = 62 * 2**20


def place():
    dp, seq = lax.axis_index("dp"), lax.axis_index("seq")
    return lax.rem(dp, SIDE), lax.div(dp, SIDE), lax.div(seq, 2), lax.rem(seq, 2)


def wrap(value, size=SIDE):
    return lax.rem(value + size, size)


def at(x, y, z, core):
    return (y * SIDE + x, z * 2 + core)


class Copies:
    def __init__(self, send, recv):
        self.send, self.recv, self.started, self.sent = send, recv, [], set()

    def plan(self, source, target, device):
        index = len(self.started)
        assert index < self.send.shape[0]
        copy = pltpu.make_async_remote_copy(
            src_ref=source,
            dst_ref=target,
            send_sem=self.send.at[index],
            recv_sem=self.recv.at[index],
            device_id=device,
            device_id_type=MESH,
        )
        self.started.append(copy)
        return copy

    def start(self, source, target, device):
        copy = self.plan(source, target, device)
        copy.start()
        return copy

    def drain(self, some=None):
        for copy in self.started if some is None else some:
            if id(copy) not in self.sent:
                self.sent.add(id(copy))
                copy.wait_send()


def seq_peers(x, y, z, core):
    seq = z * 2 + core
    return [(y * SIDE + x, wrap(seq + k, PEERS)) for k in range(1, PEERS)]


def halver(dim, low):
    def split(ref, part):
        size = ref.shape[dim]
        places = [slice(None)] * len(ref.shape)
        places[dim] = pl.ds(0, low) if part == 0 else pl.ds(low, size - low)
        return ref.at[tuple(places)]

    return split


class RingGather:
    def __init__(self, copies, me, to, block, split):
        self.copies, self.me, self.to, self.block, self.split = copies, me, to, block, split

    def plan(self, source=None):
        source = self.block(self.me) if source is None else source
        below, above = wrap(self.me - 1), wrap(self.me + 1)

        def move(start, target, part, place):
            return self.copies.plan(self.split(start, part), self.split(target, part), self.to(place))

        mine, before, after = self.block(self.me), self.block(below), self.block(above)
        self.up = [move(source, mine, part, above) for part in range(2)]
        self.down = [move(source, mine, part, below) for part in range(2)]
        self.pass_up = move(before, before, 0, above)
        self.pass_down = move(after, after, 1, below)

    def first(self, source=None):
        if not hasattr(self, "up"):
            self.plan(source)
        self.up[0].start()
        self.down[1].start()
        self.up[1].start()
        self.down[0].start()

    def second(self):
        self.up[0].wait_recv()
        self.pass_up.start()
        self.down[1].wait_recv()
        self.pass_down.start()

    def wait_below(self):
        self.up[1].wait_recv()

    def wait_above(self):
        self.down[0].wait_recv()

    def wait_far(self):
        self.pass_up.wait_recv()
        self.pass_down.wait_recv()

    def finish(self):
        self.wait_below()
        self.wait_above()
        self.wait_far()

    def copies_made(self):
        return [*self.up, *self.down, self.pass_up, self.pass_down]


class RingReduce:
    def __init__(self, copies, me, to, block, split, landing):
        self.copies, self.me, self.to, self.block, self.split = copies, me, to, block, split
        self.low_in, self.high_in, self.plus_in, self.minus_in = landing

    def plan(self):
        far, below, above = wrap(self.me + 2), wrap(self.me - 1), wrap(self.me + 1)
        plan, split = self.copies.plan, self.split
        self.far_up = plan(split(self.block(far), 0), self.low_in, self.to(above))
        self.far_down = plan(split(self.block(far), 1), self.high_in, self.to(below))
        self.up = [plan(split(self.block(above), k), split(self.plus_in, k), self.to(above)) for k in range(2)]
        self.down = [plan(split(self.block(below), k), split(self.minus_in, k), self.to(below)) for k in range(2)]

    def first_far(self):
        self.far_up.start()
        self.far_down.start()

    def first_above(self):
        self.up[1].start()

    def first_below(self):
        self.down[0].start()

    def first(self):
        if not hasattr(self, "up"):
            self.plan()
        self.first_far()
        self.first_above()
        self.first_below()

    def second(self):
        below, above = self.block(wrap(self.me - 1)), self.block(wrap(self.me + 1))
        self.far_up.wait_recv()
        accumulate(self.split(above, 0), self.split(above, 0), self.low_in)
        self.up[0].start()
        self.far_down.wait_recv()
        accumulate(self.split(below, 1), self.split(below, 1), self.high_in)
        self.down[1].start()

    def copies_made(self):
        return [self.far_up, self.far_down, *self.up, *self.down]

    def finish(self, target=None):
        own = self.block(self.me)
        for copy in (*self.up, *self.down):
            copy.wait_recv()
        accumulate(own if target is None else target, own, self.plus_in, self.minus_in)


def accumulate(target, *sources):
    shape = target.shape
    if len(shape) > 2:
        for index in range(shape[0]):
            accumulate(target.at[index], *[source.at[index] for source in sources])
        return
    step = 16

    @pl.loop(0, shape[0] // step)
    def _(i):
        rows = pl.ds(pl.multiple_of(i * step, step), step)
        total = sources[0][rows, :].astype(F32)
        for source in sources[1:]:
            total = total + source[rows, :].astype(F32)
        target[rows, :] = total.astype(target.dtype)


def columns_of(seq, dp_count=16):
    return [(288 * d + OWN * seq, 36 * d) for d in range(dp_count)]


def dot(a, b, dims=((1,), (0,))):
    return lax.dot_general(a, b, (dims, ((), ())), preferred_element_type=F32)


NT = ((1,), (1,))
TN = ((0,), (0,))
ROWS = 256
PAIR = 512
EVERY = 272
HALF = 512


def by_rows(ref, which, part):
    start, size = (32 * which, 32) if part is None else (32 * which + 16 * part, 16)
    lead = [slice(None)] * (len(ref.shape) - 2)
    return ref.at[(*lead, pl.ds(start, size), slice(None))]


def by_columns(ref, which, part):
    first, size = ((0, 1152), (0, 640), (640, 512))[0 if part is None else part + 1]
    lead = [slice(None)] * (len(ref.shape) - 2)
    return ref.at[(*lead, slice(None), pl.ds(1152 * which + first, size))]


def visit(z, k):
    return wrap(z + k + lax.div(k, 2) * (5 - 2 * k))


def turn_of(z, chip):
    ahead = wrap(chip - z)
    return ahead + lax.div(ahead, 2) * (5 - 2 * ahead)


class PlaneGather:
    def __init__(self, copies, spot, view, halves, block, split):
        x, y, z, core = spot
        to_x, to_y = (lambda i: at(i, y, z, core)), (lambda i: at(x, i, z, core))
        everything, fours = slice(None), halver(0, 2)
        self.x, self.y, self.view, self.halves = x, y, view, halves
        self.row_x = RingGather(copies, x, to_x, lambda i: halves(view(y, i), 0, None), split)
        self.row_y = RingGather(copies, y, to_y, lambda i: halves(view(i, x), 1, None), split)
        self.all_y = RingGather(copies, y, to_y, lambda i: halves(view(i, everything), 0, None), fours)
        self.all_x = RingGather(copies, x, to_x, lambda i: halves(view(everything, i), 1, None), fours)
        self.row_x.plan(halves(block, 0, None))
        self.row_y.plan(halves(block, 1, None))
        self.all_y.plan()
        self.all_x.plan()

    def one(self):
        self.row_x.first()
        self.row_y.first()

    def two(self):
        self.row_x.second()
        self.row_y.second()

    def three(self):
        self.row_x.finish()
        self.all_y.first()
        self.row_y.finish()
        self.all_x.first()

    def four(self):
        self.all_y.second()
        self.all_x.second()

    def finish(self):
        self.all_y.finish()
        self.all_x.finish()

    def copies(self):
        return [copy for ring in (self.row_x, self.row_y, self.all_y, self.all_x) for copy in ring.copies_made()]

    def group(self, which, step):
        everything = slice(None)
        if which == 0:
            return self.halves(self.view(wrap(self.y + step), everything), 0, None)
        return self.halves(self.view(everything, wrap(self.x + step)), 1, None)


ORDERS = (("x", "y", "z"), ("y", "z", "x"), ("z", "x", "y"))


def cube_spots(spot, order):
    x, y, z, core = spot
    own = {"x": x, "y": y, "z": z}
    to = {
        "x": lambda i: at(i, y, z, core),
        "y": lambda i: at(x, i, z, core),
        "z": lambda i: at(x, y, i, core),
    }

    def view(ref, **places):
        return ref.at[tuple(places.get(axis, own[axis]) for axis in ("y", "x", "z"))]

    return [own[axis] for axis in order], [to[axis] for axis in order], view


def cube_rings(spot, order, ref, make):
    (a, b, c), (to_a, to_b, to_c), view = cube_spots(spot, order)
    one, two, three = order
    everything = slice(None)
    place_of = {"y": 0, "x": 1, "z": 2}
    first = make(a, to_a, lambda i: view(ref, **{one: i}), halver(-1, ref.shape[-1] // 2))
    second = make(b, to_b, lambda i: view(ref, **{one: everything, two: i}), halver(0, 2))
    third = make(
        c, to_c,
        lambda i: view(ref, **{one: everything, two: everything, three: i}),
        halver(0 if place_of[two] < place_of[one] else 1, 2),
    )
    return first, second, third


def small_rows(small_all):
    pieces = [small_all[d // 4, d % 4][:, :64] for d in range(16)]
    return jnp.concatenate(pieces, axis=1)


def normalize(rows, gain):
    inverse = lax.rsqrt(jnp.mean(rows * rows, axis=-1, keepdims=True) + epsilon_norm)
    return rows * inverse * gain


def extend(extended, projected, half, sequence):
    first = pl.ds(ROWS + 8 * sequence, 8)
    main = pl.ds(128 * sequence, 128)
    extended[0:8, :] = projected[half, first, :HALF] * projected[half, first, 1024:]
    extended[8:136, :] = projected[half, main, :HALF] * projected[half, main, 1024:]


def convolve(extended, taps):
    return taps[0:1] * extended[6:134, :] + taps[1:2] * extended[7:135, :] + taps[2:3] * extended[8:136, :]


def half_lanes(half):
    return pl.ds(pl.multiple_of(half * HALF, HALF), HALF)


class PlaneReduce:
    def __init__(self, copies, spot, view, halves, split, landings):
        x, y, z, core = spot
        to_x, to_y = (lambda i: at(i, y, z, core)), (lambda i: at(x, i, z, core))
        everything, fours = slice(None), halver(0, 2)
        self.halves = halves
        self.all_y = RingReduce(copies, y, to_y, lambda i: halves(view(i, everything), 0, None), fours, landings[0:4])
        self.all_x = RingReduce(copies, x, to_x, lambda i: halves(view(everything, i), 1, None), fours, landings[4:8])
        self.row_x = RingReduce(copies, x, to_x, lambda i: halves(view(y, i), 0, None), split, landings[8:12])
        self.row_y = RingReduce(copies, y, to_y, lambda i: halves(view(i, x), 1, None), split, landings[12:16])

    def one(self):
        self.all_y.first()
        self.all_x.first()

    def two(self):
        self.all_y.second()
        self.all_x.second()

    def three(self):
        self.all_y.finish()
        self.row_x.first()
        self.all_x.finish()
        self.row_y.first()

    def four(self):
        self.row_x.second()
        self.row_y.second()

    def finish(self, target):
        self.row_x.finish(self.halves(target, 0, None))
        self.row_y.finish(self.halves(target, 1, None))


def plane_landings(ref):
    wide = lambda count, blocks, rows: ref.reshape(count, blocks, rows, 1152)
    single = lambda rows: ref.reshape(2048 // rows, rows, 1152)
    fed, downs = [], []
    for k in range(2):
        fed += [wide(32, 2, 32).at[8 + 2 * k], wide(32, 2, 32).at[9 + 2 * k]]
        fed += [wide(16, 4, 32).at[2 * k], wide(16, 4, 32).at[2 * k + 1]]
        downs += [wide(64, 2, 16).at[38 + 2 * k], wide(64, 2, 16).at[39 + 2 * k]]
        downs += [wide(32, 4, 16).at[15 + 2 * k], wide(32, 4, 16).at[16 + 2 * k]]
    for k in range(2):
        fed += [single(16).at[56 + 2 * k], single(16).at[57 + 2 * k], single(32).at[24 + 2 * k], single(32).at[25 + 2 * k]]
        downs += [single(16).at[88 + 2 * k, :, pl.ds(0, 640)], single(16).at[89 + 2 * k, :, pl.ds(0, 512)]]
        downs += [single(16).at[84 + 2 * k], single(16).at[85 + 2 * k]]
    return fed, downs


def cube_landings(ref, order):
    width = ref.shape[-1]
    place_of = {"y": 0, "x": 1, "z": 2}
    halved = (2, 4) if place_of[order[1]] < place_of[order[0]] else (4, 2)
    single, half = ref.reshape(64, 16, width), pl.ds(0, width // 2)
    first = [single.at[60, :, half], single.at[61, :, half], single.at[62], single.at[63]]
    pairs, fours = ref.reshape(32, 2, 16, width), ref.reshape(16, 4, 16, width)
    second = [pairs.at[24], pairs.at[25], fours.at[13], fours.at[14]]
    lows, wholes = ref.reshape(8, *halved, 16, width), ref.reshape(4, 4, 4, 16, width)
    third = [lows.at[4], lows.at[5], wholes.at[0], wholes.at[1]]
    return first, second, third


def local_copies(semaphores):
    count = iter(range(semaphores.shape[0]))

    def start(source, target):
        copy = pltpu.make_async_copy(source, target, semaphores.at[next(count)])
        copy.start()
        return copy

    return start


OPERANDS = ("w_in", "w_out", "w_gate", "w_up", "w_down", "gains", "taps", "inputs", "cotangent")
RESULTS = {
    "output": ((2, 128, D), BF),
    "input_grad": ((2, 128, D), F32),
    "g_in": ((8, 3072), F32),
    "g_out": ((8, 1024), F32),
    "g_gate": ((8, 4608), F32),
    "g_up": ((8, 4608), F32),
    "g_down": ((OWN, D), F32),
    "g_small": ((8, 128), F32),
}
SCRATCH = {
    "w_in": ((8, 3072), F32),
    "w_out": ((8, 1024), F32),
    "w_gate": ((8, 4608), F32),
    "w_up": ((8, 4608), F32),
    "w_down": ((OWN, D), F32),
    "tile": ((8, 128), F32),
    "inputs": ((2, 128, D), BF),
    "mix": ((2, 4, 4, 64, 2048), BF),
    "feed": ((4, 4, 64, 2 * SLICE), BF),
    "down": ((4, 4, 16, PACKED), BF),
    "small_all": ((4, 4, 8, 128), F32),
    "edge_in": ((2, 16, D), BF),
    "tokens": ((SIDE, 2, ROWS, D), BF),
    "grads": ((SIDE, 2, ROWS, D), BF),
    "mix_send": ((2, 16, D), BF),
    "feed_send": ((PEERS, 16, 640), BF),
    "mix_got": ((PEERS, 16, D), BF),
    "feed_got": ((PEERS, 16, 640), BF),
    "small_got": ((PEERS, 8, 128), F32),
    "mix_block": ((64, 2048), BF),
    "feed_block": ((64, 2 * SLICE), BF),
    "down_block": ((16, PACKED), BF),
    "small_send": ((8, 128), F32),
    "rows": ((8, D), F32),
    "normed": ((EVERY, D), BF),
    "projected": ((2, EVERY, 1536), F32),
    "extended": ((136, HALF), F32),
    "mixer_in": ((ROWS, D), BF),
    "hidden": ((ROWS, D), F32),
    "normed_two": ((ROWS, D), BF),
    "down_rows": ((SLICE, D), BF),
    "narrow_wide": ((160, D), F32),
    "value": ((PAIR, 2 * SLICE), F32),
    "grad_active": ((PAIR, SLICE), F32),
    "active": ((2048, SLICE), BF),
    "grad_value": ((2048, 2 * SLICE), BF),
    "part": ((SIDE, 2, ROWS, D), BF),
    "part_out": ((SIDE, 2, ROWS, D), BF),
    "landing": ((SIDE, ROWS, D), BF),
    "landing_left": ((SIDE, ROWS, HALF), BF),
    "landing_right": ((SIDE, ROWS, HALF), BF),
    "low_in": ((128, D), BF),
    "high_in": ((128, D), BF),
    "plus_in": ((ROWS, D), BF),
    "minus_in": ((ROWS, D), BF),
    "low_out": ((128, D), BF),
    "high_out": ((128, D), BF),
    "plus_out": ((ROWS, D), BF),
    "minus_out": ((ROWS, D), BF),
    "down_part": ((SLICE, 256), F32),
    "down_tail": ((16, 16, 256), F32),
    "grad_conv": ((2, 136, D), F32),
    "grad_x": ((2, ROWS, HALF), BF),
    "edge_send": ((2, 8, D), F32),
    "edge_got": ((2, 8, D), F32),
    "sums": ((8, D), F32),
    "mix_wide": ((16, 2048), F32),
    "feed_wide": ((64, 2 * SLICE), F32),
    "down_wide": ((16, PACKED), F32),
    "mix_land": ((2, 8, 2048), F32),
    "feed_land": ((PEERS, 8, 2 * SLICE), F32),
    "small": ((4, 4, 8, 128), F32),
    "small_y": ((4, 4, 8, 128), F32),
    "small_x": ((4, 8, 128), F32),
    "small_z": ((PEERS, 8, 128), F32),
    "small_one": ((4, 8, 128), F32),
    "small_two": ((8, 128), F32),
    "g_small": ((8, 128), F32),
}
COPIES = 352


def step_kernel(*refs):
    count = len(OPERANDS)
    given = types.SimpleNamespace(**dict(zip(OPERANDS, refs)))
    result = types.SimpleNamespace(**dict(zip(RESULTS, refs[count:])))
    count += len(RESULTS)
    m = types.SimpleNamespace(**dict(zip(SCRATCH, refs[count:])))
    ready, load_sem, save_sem, send, recv = refs[count + len(SCRATCH) :]

    spot = x, y, z, core = place()
    seq = z * 2 + core
    copies = Copies(send, recv)
    peers = seq_peers(x, y, z, core)
    across = [at(wrap(x + k), y, z, core) for k in range(1, SIDE)]
    along = [at(x, wrap(y + k), z, core) for k in range(1, SIDE)]
    partner = at(x, y, z, 1 - core)
    load = local_copies(load_sem)
    loads = {
        "w_in": load(given.w_in, m.w_in),
        "w_out": load(given.w_out, m.w_out),
        "w_gate": load(given.w_gate, m.w_gate),
        "w_up": load(given.w_up, m.w_up),
        "w_down": load(given.w_down, m.w_down),
        "inputs": load(given.inputs, m.inputs),
        "cotangent": load(given.cotangent, m.grads.at[z, core]),
    }
    barrier = pltpu.get_barrier_semaphore()
    for device in peers + across + along:
        pl.semaphore_signal(barrier, inc=1, device_id=device, device_id_type=MESH)

    def to_z(i):
        return at(x, y, i, core)

    loads["w_in"].wait()
    loads["w_out"].wait()
    for half in range(2):
        parts = [m.w_out[:, 512 * half : 512 * half + 512]]
        parts += [m.w_in[:, 1024 * k + 512 * half : 1024 * k + 512 * half + 512] for k in range(3)]
        upper = jnp.concatenate(parts[:2], axis=1)
        lower = jnp.concatenate(parts[2:], axis=1)
        m.mix_send[half] = jnp.concatenate([upper, lower], axis=0).astype(BF)
    pl.semaphore_wait(barrier, len(peers + across + along))
    mix_copies = []
    for k, peer in enumerate(peers):
        other = wrap(seq + k + 1, PEERS)
        mix_copies.append(copies.start(m.mix_send.at[lax.rem(other, 2)], m.mix_got.at[seq], peer))
    m.mix_got[seq] = m.mix_send[core]
    m.tile[...] = jnp.zeros_like(m.tile)
    m.tile[0:2, 0:8] = given.gains[...].astype(BF).astype(F32)
    m.tile[2:5, 0:8] = given.taps[...].astype(BF).astype(F32)
    m.small_got[seq] = pltpu.roll(m.tile[...], seq * 8, 1)
    small_copies = [copies.start(m.small_got.at[seq], m.small_got.at[seq], peer) for peer in peers]
    edge_copy = copies.start(
        given.inputs.at[:, pl.ds(112, 16)], m.edge_in, (y * SIDE + x, wrap(seq + 1, PEERS))
    )
    mixed = PlaneGather(copies, spot, lambda i, j: m.mix.at[core, i, j], by_rows, m.mix_block, halver(-2, 16))
    fed = PlaneGather(copies, spot, lambda i, j: m.feed.at[i, j], by_rows, m.feed_block, halver(-2, 16))
    downs = PlaneGather(copies, spot, lambda i, j: m.down.at[i, j], by_columns, m.down_block, halver(-1, 640))
    ring = RingGather(
        copies, z, to_z,
        lambda i: m.grads.at[i, core],
        halver(0, 128),
    )
    ring.plan(given.cotangent)

    for copy in mix_copies:
        copy.wait_recv()
    for k in range(4):
        a, b = m.mix_got[2 * k].astype(F32), m.mix_got[2 * k + 1].astype(F32)
        line = slice(16 * k, 16 * k + 16)
        m.mix_block[line, :1024] = jnp.concatenate([a[:8], b[:8]], axis=0).astype(BF)
        m.mix_block[line, 1024:] = jnp.concatenate([a[8:], b[8:]], axis=0).astype(BF)
    mixed.one()
    m.mix[core, y, x] = m.mix_block[...]
    ring.first()
    cotangent_ring = ring
    grads_passed = [copies.start(given.cotangent, m.grads.at[z, core], partner)]

    def slices(which):
        for s in which:
            gate = jnp.concatenate([m.w_gate[:, a : a + OWN] for a, _ in columns_of(s)], axis=1)
            up = jnp.concatenate([m.w_up[:, a : a + OWN] for a, _ in columns_of(s)], axis=1)
            tail = jnp.concatenate([gate[:, WIDE:], up[:, WIDE:]], axis=1)
            upper = jnp.concatenate([gate[:, :WIDE], up[:, :128]], axis=1)
            lower = jnp.concatenate([up[:, 128:WIDE], tail, jnp.zeros((8, 128), F32)], axis=1)
            m.feed_send[s] = jnp.concatenate([upper, lower], axis=0).astype(BF)

    loads["w_gate"].wait()
    loads["w_up"].wait()
    slices(range(0, 4))
    mixed.two()
    slices(range(4, 8))
    feed_copies = []
    for k, peer in enumerate(peers):
        other = wrap(seq + k + 1, PEERS)
        feed_copies.append(copies.start(m.feed_send.at[other], m.feed_got.at[seq], peer))
    m.feed_got[seq] = m.feed_send[seq]
    for copy in small_copies:
        copy.wait_recv()
    m.small_send[...] = functools.reduce(lambda a, b: a + b, [m.small_got[s] for s in range(PEERS)])
    small_x = [copies.start(m.small_send, m.small_all.at[y, x], device) for device in across]
    m.small_all[y, x] = m.small_send[...]
    mixed.three()
    mix_passed = []

    def pass_on(step):
        for which in range(2):
            part = mixed.group(which, step)
            mix_passed.append(copies.start(part, part, partner))

    pass_on(0)
    for copy in small_x:
        copy.wait_recv()
    small_y = [copies.start(m.small_all.at[y], m.small_all.at[y], device) for device in along]
    loads["w_down"].wait()
    for i in range(4):
        m.narrow_wide[4 * i : 4 * i + 4, 0:256] = m.w_down[32:36, 256 * i : 256 * i + 256]
    m.down_block[:, 0:1024] = m.w_down[0:16, :].astype(BF)
    m.down_block[:, 1024:2048] = m.w_down[16:32, :].astype(BF)
    m.down_block[:, 2048:PACKED] = m.narrow_wide[0:16, 0:256].astype(BF)
    m.down[y, x] = m.down_block[...]
    for copy in feed_copies:
        copy.wait_recv()
    for k in range(4):
        a, b = m.feed_got[2 * k].astype(F32), m.feed_got[2 * k + 1].astype(F32)
        line = slice(16 * k, 16 * k + 16)
        m.feed_block[line, :640] = jnp.concatenate([a[:8], b[:8]], axis=0).astype(BF)
        m.feed_block[line, 640:] = jnp.concatenate([a[8:, :512], b[8:, :512]], axis=0).astype(BF)
    m.feed[y, x] = m.feed_block[...]
    for copy in small_y:
        copy.wait_recv()
    m.rows[...] = small_rows(m.small_all)
    loads["inputs"].wait()
    for q in range(2):
        m.normed[128 * q : 128 * q + 128, :] = normalize(m.inputs[q].astype(F32), m.rows[0:1, :]).astype(BF)
    edge_copy.wait_recv()
    inside = (seq > 0).astype(F32)
    earlier = [normalize(m.edge_in[q].astype(F32)[8:], m.rows[0:1, :]) * inside for q in range(2)]
    m.normed[ROWS:EVERY, :] = jnp.concatenate(earlier, axis=0).astype(BF)
    ring.second()
    mixed.four()
    downs.one()
    fed.one()
    mixed.all_y.wait_below()
    mixed.all_x.wait_below()
    pass_on(-1)
    mixed.all_y.wait_above()
    mixed.all_x.wait_above()
    pass_on(1)
    downs.two()
    fed.two()
    downs.three()
    fed.three()
    mixed.all_y.wait_far()
    mixed.all_x.wait_far()
    pass_on(2)
    ring.finish()
    for step in (1, 3, 2):
        chunk = m.grads.at[wrap(z + step), core]
        grads_passed.append(copies.start(chunk, chunk, partner))

    for turn in range(2):
        if turn == 1:
            for copy in mix_passed:
                copy.wait_recv()
        half = core if turn == 0 else 1 - core
        m.projected[half] = dot(m.normed[...], m.mix.at[half].reshape(D, 2048)[:, HALF:])
        lanes = half_lanes(half)
        for q in range(2):
            main = slice(128 * q, 128 * q + 128)
            extend(m.extended, m.projected, half, q)
            convolved = convolve(m.extended, m.rows[2:5, lanes])
            m.mixer_in[main, lanes] = (m.projected[half, main, HALF:1024] * convolved).astype(BF)
    weights = [m.mix.at[half].reshape(D, 2048) for half in range(2)]
    for half in range(2):
        lanes = slice(HALF * half, HALF * half + HALF)
        mixed_out = dot(m.mixer_in[...], weights[half][:, :HALF])
        for q in range(2):
            main = slice(128 * q, 128 * q + 128)
            m.hidden[main, lanes] = m.inputs[q, :, lanes].astype(F32) + mixed_out[main]
    m.normed_two[...] = normalize(m.hidden[...], m.rows[1:2, :]).astype(BF)

    around = RingGather(
        copies, z, to_z,
        lambda i: m.tokens.at[i, core],
        halver(0, 128),
    )
    around.plan(m.normed_two)
    passed = [copies.plan(m.normed_two, m.tokens.at[z, core], partner)]
    for step in (1, 3, 2):
        chunk = m.tokens.at[wrap(z + step), core]
        passed.append(copies.plan(chunk, chunk, partner))
    around.first()
    passed[0].start()
    m.tokens[z, core] = m.normed_two[...]
    downs.four()
    fed.four()
    gives, gives_left, gives_right = [], [], []
    for k in range(SIDE):
        theirs = m.part_out.at[k, 1 - core]
        gives.append(copies.plan(m.part.at[k, 1 - core], m.landing.at[k], partner))
        gives_left.append(copies.plan(theirs.at[:, 0:HALF], m.landing_left.at[k], partner))
        gives_right.append(copies.plan(theirs.at[:, HALF:D], m.landing_right.at[k], partner))
    reduce = RingReduce(
        copies, z, to_z,
        lambda i: m.part.at[turn_of(z, i), core],
        halver(0, 128),
        (m.low_in, m.high_in, m.plus_in, m.minus_in),
    )
    reduce.plan()
    downs.finish()
    for i in range(SIDE):
        for d in range(SIDE):
            packed = m.down[i, d].astype(F32)
            m.narrow_wide[OWN * d : OWN * d + 16, :] = packed[:, 0:1024]
            m.narrow_wide[OWN * d + 16 : OWN * d + 32, :] = packed[:, 1024:2048]
            for k in range(4):
                m.narrow_wide[OWN * d + 32 : OWN * d + 36, 256 * k : 256 * k + 256] = packed[4 * k : 4 * k + 4, 2048:]
        m.down_rows[144 * i : 144 * i + 144, :] = m.narrow_wide[0:144, :].astype(BF)
    for copy in grads_passed:
        copy.wait_recv()
    loads["cotangent"].wait()
    fed.finish()
    feed = m.feed.reshape(D, 2 * SLICE)
    around.second()
    around.wait_above()
    passed[1].start()
    around.wait_below()
    passed[2].start()

    @pl.loop(0, SIDE)
    def _(k):
        @pl.when(k == 0)
        def _():
            passed[0].wait_recv()

        @pl.when(k == 1)
        def _():
            passed[1].wait_recv()

        @pl.when(k == 2)
        def _():
            passed[2].wait_recv()
            around.wait_far()
            passed[3].start()

        @pl.when(k == 3)
        def _():
            passed[3].wait_recv()

        chip = visit(z, k)
        m.value[...] = dot(m.tokens.at[chip].reshape(PAIR, D)[...], feed[...])
        m.grad_active[...] = dot(m.grads.at[chip].reshape(PAIR, D)[...], m.down_rows[...], NT)
        base = chip * PAIR

        @pl.loop(0, PAIR // 64)
        def _(r):
            line = pl.ds(pl.multiple_of(r * 64, 64), 64)
            target = pl.ds(pl.multiple_of(base + r * 64, 64), 64)
            tail = m.value[line, 1024:1152]
            ends = []
            for gate, up, back, where in (
                (m.value[line, :WIDE], m.value[line, WIDE:1024], m.grad_active[line, :WIDE], slice(0, WIDE)),
                (tail[:, :64], tail[:, 64:], m.grad_active[line, WIDE:], slice(WIDE, SLICE)),
            ):
                sigmoid = jax.nn.sigmoid(gate)
                soft = gate * sigmoid
                m.active[target, where] = (soft * up).astype(BF)
                grad_up = (back * soft).astype(BF)
                grad_gate = (back * up * (sigmoid * (1.0 + gate * (1.0 - sigmoid)))).astype(BF)
                ends.append((grad_gate, grad_up))
            m.grad_value[target, :WIDE] = ends[0][0]
            m.grad_value[target, WIDE:1024] = ends[0][1]
            m.grad_value[target, 1024:1088] = ends[1][0]
            m.grad_value[target, 1088:1152] = ends[1][1]

        lines = pl.ds(pl.multiple_of(base, PAIR), PAIR)
        m.part.at[k].reshape(PAIR, D)[...] = dot(m.grad_value[lines, :], feed[...], NT).astype(BF)
        for step in range(SIDE):
            @pl.when(k == step)
            def _(step=step):
                gives[step].start()
        m.part_out.at[k].reshape(PAIR, D)[...] = dot(m.active[lines, :], m.down_rows[...]).astype(BF)
        for step in range(SIDE):
            @pl.when(k == step)
            def _(step=step):
                gives_left[step].start()
                gives_right[step].start()
                gives[step].wait_recv()
                accumulate(m.part.at[step, core], m.part.at[step, core], m.landing.at[step])
                if step == 1:
                    reduce.first_above()
                if step == 2:
                    reduce.first_below()
                if step == 3:
                    reduce.first_far()

    copies.drain(fed.copies())
    copies.drain(downs.copies())
    every_grad, every_token = m.grads.reshape(2048, D), m.tokens.reshape(2048, D)

    @pl.loop(0, 4)
    def _(n):
        columns = pl.ds(pl.multiple_of(n * 256, 256), 256)
        feed[columns, :] = dot(every_token[:, columns], m.grad_value[...], TN).astype(BF)

    plane_neighbours = [at(wrap(x + 1), y, z, core), at(wrap(x - 1), y, z, core)]
    plane_neighbours += [at(x, wrap(y + 1), z, core), at(x, wrap(y - 1), z, core)]
    for device in plane_neighbours:
        pl.semaphore_signal(ready.at[0], inc=1, device_id=device, device_id_type=MESH)
    reduce.second()

    def down_columns(n):
        columns = slice(256 * n, 256 * n + 256)
        m.down_part[...] = dot(m.active[...], every_grad[:, columns], TN)
        for d in range(16):
            block = m.down.at[d // 4, d % 4]
            block[:, columns] = m.down_part[OWN * d : OWN * d + 16, :].astype(BF)
            block[:, 1024 + 256 * n : 1280 + 256 * n] = m.down_part[OWN * d + 16 : OWN * d + 32, :].astype(BF)
            m.down_tail[d, 4 * n : 4 * n + 4, :] = m.down_part[OWN * d + 32 : OWN * d + 36, :]

    fed_landings, down_landings = plane_landings(m.grad_value)
    fed = PlaneReduce(copies, spot, lambda i, j: m.feed.at[i, j], by_rows, halver(-2, 16), fed_landings)
    downs = PlaneReduce(copies, spot, lambda i, j: m.down.at[i, j], by_columns, halver(-1, 640), down_landings)
    down_columns(0)
    pl.semaphore_wait(ready.at[0], len(plane_neighbours))
    fed.one()
    for n in range(1, 4):
        down_columns(n)
    for d in range(16):
        m.down[d // 4, d % 4, :, 2048:PACKED] = m.down_tail[d].astype(BF)
    downs.one()
    for k in range(SIDE):
        gives_left[k].wait_recv()
        gives_right[k].wait_recv()
        ours = m.part_out.at[k, core]
        accumulate(ours.at[:, 0:HALF], ours.at[:, 0:HALF], m.landing_left.at[k])
        accumulate(ours.at[:, HALF:D], ours.at[:, HALF:D], m.landing_right.at[k])
    ring = RingReduce(
        copies, z, to_z,
        lambda i: m.part_out.at[turn_of(z, i), core],
        halver(0, 128),
        (m.low_out, m.high_out, m.plus_out, m.minus_out),
    )
    ring.first()
    grad_hidden = m.value.at[0:ROWS, 0:D]
    grad_mixer = m.value.at[ROWS : 2 * ROWS, 0:D]
    reduce.finish(grad_hidden)

    copies.drain(gives + gives_left + gives_right + reduce.copies_made() + around.copies_made() + passed)
    copies.drain(grads_passed)
    copies.drain(cotangent_ring.copies_made())
    neighbours = plane_neighbours + [at(x, y, wrap(z + 1), core), at(x, y, wrap(z - 1), core), partner]
    for device in neighbours:
        pl.semaphore_signal(ready.at[1], inc=1, device_id=device, device_id_type=MESH)

    sum_blocks = m.grads.reshape(2, 4, 4, 4, 16, D)
    sum_views = [sum_blocks.at[0]] + [sum_blocks.at[1, :, :, :, :, pl.ds(HALF * k, HALF)] for k in range(2)]

    def flat_views(ref):
        flat = ref.reshape(2, D, D)
        return [flat.at[0], flat.at[1, :, pl.ds(0, HALF)], flat.at[1, :, pl.ds(HALF, HALF)]]

    sum_flat, give_flat, got_flat = flat_views(m.grads), flat_views(m.tokens), flat_views(m.part)
    cubes = []
    for ref, buffer, order in zip(sum_views, (m.landing, m.landing_left, m.landing_right), ORDERS):
        lands = iter(cube_landings(buffer, order))

        def make(me, to, block, split, lands=lands):
            return RingReduce(copies, me, to, block, split, next(lands))

        cubes.append(cube_rings(spot, order, ref, make))
    save = local_copies(save_sem)
    saves = []

    m.sums[...] = jnp.zeros_like(m.sums)
    narrow = m.normed_two

    @pl.loop(0, 8)
    def _(n):
        line = pl.ds(pl.multiple_of(n * 32, 32), 32)
        tokens = m.hidden[line, :]
        inverse = lax.rsqrt(jnp.mean(tokens * tokens, axis=-1, keepdims=True) + epsilon_norm)
        scaled = tokens * inverse
        upstream = grad_hidden[line, :]
        m.sums[1:2, :] += jnp.sum(upstream * scaled, axis=0, keepdims=True)
        weighted = upstream * m.rows[1:2, :]
        total = m.grads[z, core, line, :].astype(F32) + inverse * (
            weighted - scaled * jnp.mean(weighted * scaled, axis=-1, keepdims=True)
        )
        grad_hidden[line, :] = total
        narrow[line, :] = total.astype(BF)

    grad_mixer[...] = dot(narrow[:, :HALF], weights[0][:, :HALF], NT) + dot(narrow[:, HALF:], weights[1][:, :HALF], NT)
    for q in range(2):
        for half in range(2):
            lanes = slice(HALF * half, HALF * half + HALF)
            start = slice(128 * q, 128 * q + 8)
            m.edge_send[q, :, lanes] = grad_mixer[start, lanes] * m.projected[half, start, HALF:1024]
    edge_copy = copies.start(m.edge_send, m.edge_got, (y * SIDE + x, wrap(seq - 1, PEERS)))
    fed.two()
    grad_bc = m.grad_value.reshape(8, ROWS, 2 * SLICE)
    for half in range(2):
        lanes = slice(HALF * half, HALF * half + HALF)
        for q in range(2):
            main = slice(128 * q, 128 * q + 128)
            extend(m.extended, m.projected, half, q)
            upstream = grad_mixer[main, lanes]
            grad_bc[6 + half, main, HALF:D] = (upstream * convolve(m.extended, m.rows[2:5, lanes])).astype(BF)
            back = upstream * m.projected[half, main, HALF:1024]
            m.grad_conv[q, 0:128, lanes] = back
            for k in range(3):
                m.sums[2 + k : 3 + k, lanes] += jnp.sum(back * m.extended[6 + k : 134 + k, :], axis=0, keepdims=True)
    ring.second()
    edge_copy.wait_recv()
    inside = (seq < PEERS - 1).astype(F32)
    for q in range(2):
        m.grad_conv[q, 128:136, :] = m.edge_got[q] * inside
        main = slice(128 * q, 128 * q + 128)
        for half in range(2):
            lanes = slice(HALF * half, HALF * half + HALF)
            taps = m.rows[2:5, lanes]
            gated = (
                taps[2:3] * m.grad_conv[q, 0:128, lanes]
                + taps[1:2] * m.grad_conv[q, 1:129, lanes]
                + taps[0:1] * m.grad_conv[q, 2:130, lanes]
            )
            grad_bc[6 + half, main, 0:HALF] = (gated * m.projected[half, main, 1024:]).astype(BF)
            m.grad_x[half, main, :] = (gated * m.projected[half, main, :HALF]).astype(BF)
    downs.two()

    before = m.normed.at[0:ROWS]
    given_parts = []
    for targets, half in ((give_flat, 1 - core), (sum_flat, core)):
        back, back_x, back_out = grad_bc.at[6 + half], m.grad_x.at[half], narrow.at[:, half_lanes(half)]

        @pl.loop(0, 4)
        def _(n, targets=targets, back=back, back_x=back_x, back_out=back_out):
            columns = pl.ds(pl.multiple_of(n * 256, 256), 256)
            left = before[:, columns]
            first = dot(left, back[:, 0:D], TN).astype(BF)
            targets[0][columns, HALF:D] = first[:, :HALF]
            targets[1][columns, :] = first[:, HALF:]
            targets[2][columns, :] = dot(left, back_x[...], TN).astype(BF)
            targets[0][columns, 0:HALF] = dot(m.mixer_in[:, columns], back_out[...], TN).astype(BF)

        if targets is give_flat:
            pl.semaphore_wait(ready.at[1], len(neighbours))
            for part in range(3):
                given_parts.append(copies.start(give_flat[part], got_flat[part], partner))
    for part in range(3):
        given_parts[part].wait_recv()
        accumulate(sum_flat[part], sum_flat[part], got_flat[part])
        cubes[part][2].first()
    fed.three()
    downs.three()

    grad_mixer[...] = dot(grad_bc[6, :, 0:D], weights[0][:, HALF:1536], NT)
    grad_mixer[...] += dot(grad_bc[7, :, 0:D], weights[1][:, HALF:1536], NT)
    grad_mixer[...] += dot(m.grad_x[0], weights[0][:, 1536:], NT) + dot(m.grad_x[1], weights[1][:, 1536:], NT)

    @pl.loop(0, 8)
    def _(n):
        line = pl.ds(pl.multiple_of(n * 32, 32), 32)
        tokens = m.inputs.reshape(ROWS, D)[line, :].astype(F32)
        inverse = lax.rsqrt(jnp.mean(tokens * tokens, axis=-1, keepdims=True) + epsilon_norm)
        scaled = tokens * inverse
        upstream = grad_mixer[line, :]
        m.sums[0:1, :] += jnp.sum(upstream * scaled, axis=0, keepdims=True)
        weighted = upstream * m.rows[0:1, :]
        grad_mixer[line, :] = grad_hidden[line, :] + inverse * (
            weighted - scaled * jnp.mean(weighted * scaled, axis=-1, keepdims=True)
        )

    for q in range(2):
        saves.append(save(grad_mixer.at[128 * q : 128 * q + 128], result.input_grad.at[q]))

    for part in range(3):
        cubes[part][2].second()
    fed.four()
    downs.four()

    for d in range(16):
        tile = jnp.concatenate([m.sums[:, 64 * d : 64 * d + 64], jnp.zeros((8, 64), F32)], axis=1)
        m.small[d // 4, d % 4] = tile
    sent_y = [
        copies.start(m.small.at[wrap(y + k)], m.small_y.at[k], device) for k, device in zip(range(1, SIDE), along)
    ]
    for copy in sent_y:
        copy.wait_recv()
    for i in range(SIDE):
        total = m.small[y, i]
        for k in range(1, SIDE):
            total = total + m.small_y[k, i]
        m.small_one[i] = total
    sent_x = [
        copies.start(m.small_one.at[wrap(x + k)], m.small_x.at[k], device)
        for k, device in zip(range(1, SIDE), across)
    ]
    for part in (1, 2, 0):
        cubes[part][2].finish()
        cubes[part][1].first()
    fed.finish(m.feed_wide)
    sent_feed = []
    for k, peer in enumerate(peers):
        line = pl.ds(pl.multiple_of(wrap(seq + k + 1, PEERS) * 8, 8), 8)
        sent_feed.append(copies.start(m.feed_wide.at[line], m.feed_land.at[seq], peer))
    m.feed_land[seq] = m.feed_wide[pl.ds(pl.multiple_of(seq * 8, 8), 8), :]
    downs.finish(m.down_wide)
    m.w_down[0:16, :] = m.down_wide[:, 0:1024]
    m.w_down[16:32, :] = m.down_wide[:, 1024:2048]
    for i in range(4):
        m.w_down[32:36, 256 * i : 256 * i + 256] = m.down_wide[4 * i : 4 * i + 4, 2048:PACKED]
    saves.append(save(m.w_down, result.g_down))
    for copy in sent_x:
        copy.wait_recv()
    total = m.small_one[x]
    for k in range(1, SIDE):
        total = total + m.small_x[k]
    m.small_two[...] = total
    sent_z = [copies.start(m.small_two, m.small_z.at[seq], peer) for peer in peers]
    m.small_z[seq] = total
    for part in (1, 2, 0):
        cubes[part][1].second()
    ring.finish(grad_hidden)
    m.mixer_in[...] = (m.hidden[...] + grad_hidden[...]).astype(BF)
    for q in range(2):
        saves.append(save(m.mixer_in.at[128 * q : 128 * q + 128], result.output.at[q]))
    for copy in sent_feed:
        copy.wait_recv()
    for d in range(16):
        gates, ups = [], []
        for s in range(PEERS):
            line = m.feed_land[s]
            gate = jnp.concatenate([line[:, :WIDE], line[:, 1024:1088]], axis=1)
            up = jnp.concatenate([line[:, WIDE:1024], line[:, 1088:1152]], axis=1)
            gates.append(gate[:, OWN * d : OWN * d + OWN])
            ups.append(up[:, OWN * d : OWN * d + OWN])
        m.w_gate[:, 288 * d : 288 * d + 288] = jnp.concatenate(gates, axis=1)
        m.w_up[:, 288 * d : 288 * d + 288] = jnp.concatenate(ups, axis=1)
    saves.append(save(m.w_gate, result.g_gate))
    saves.append(save(m.w_up, result.g_up))
    for copy in sent_z:
        copy.wait_recv()
    m.g_small[...] = functools.reduce(lambda a, b: a + b, [m.small_z[s] for s in range(PEERS)])
    saves.append(save(m.g_small, result.g_small))
    for part in (1, 2, 0):
        cubes[part][1].finish()
        cubes[part][0].first()
    for part in range(3):
        cubes[part][0].second()
    for part, (start, size) in enumerate(((0, D), (D, HALF), (D + HALF, HALF))):
        cubes[part][0].finish(m.mix_wide.at[:, pl.ds(start, size)])
    theirs = pl.ds(pl.multiple_of((1 - core) * 8, 8), 8)
    mix_copy = copies.start(m.mix_wide.at[theirs], m.mix_land.at[core], partner)
    m.mix_land[core] = m.mix_wide[pl.ds(pl.multiple_of(core * 8, 8), 8), :]
    mix_copy.wait_recv()
    for half in range(2):
        for k in range(3):
            m.w_in[:, 1024 * k + 512 * half : 1024 * k + 512 * half + 512] = m.mix_land[
                half, :, 512 * k + 512 : 512 * k + 1024
            ]
        m.w_out[:, 512 * half : 512 * half + 512] = m.mix_land[half, :, 0:512]
    saves.append(save(m.w_in, result.g_in))
    saves.append(save(m.w_out, result.g_out))
    for copy in saves:
        copy.wait()
    copies.drain()


def step(*operands):
    hbm, vmem = pl.BlockSpec(memory_space=pl.ANY), pl.BlockSpec(memory_space=pltpu.VMEM)
    return pl.pallas_call(
        step_kernel,
        out_shape=tuple(jax.ShapeDtypeStruct(*shape) for shape in RESULTS.values()),
        in_specs=[vmem if name in ("gains", "taps") else hbm for name in OPERANDS],
        out_specs=(hbm,) * len(RESULTS),
        scratch_shapes=[pltpu.VMEM(*shape) for shape in SCRATCH.values()]
        + [
            pltpu.SemaphoreType.REGULAR((2,)),
            pltpu.SemaphoreType.DMA((7,)),
            pltpu.SemaphoreType.DMA((10,)),
            pltpu.SemaphoreType.DMA((COPIES,)),
            pltpu.SemaphoreType.DMA((COPIES,)),
        ],
        compiler_params=pltpu.CompilerParams(
            collective_id=0, has_side_effects=True, vmem_limit_bytes=VMEM_BYTES
        ),
        name="step",
    )(*operands)


def adamw(weight, grad, first, second, rate, decay):
    first_new = beta_one * first + (1.0 - beta_one) * grad
    second_new = beta_two * second + (1.0 - beta_two) * grad * grad
    first_hat = first_new / (1.0 - beta_one**STEP)
    second_hat = second_new / (1.0 - beta_two**STEP)
    weight_new = weight - rate * (
        first_hat / (jnp.sqrt(second_hat) + epsilon_adam) + decay * weight
    )
    return (weight_new, first_new, second_new)


def shards(
    inputs, cotangent, norm_gains, conv_taps, w_in, w_out, w_gate, w_up, w_down,
    first_gains, first_taps, first_in, first_out, first_gate, first_up, first_down,
    second_gains, second_taps, second_in, second_out, second_gate, second_up, second_down,
):
    seq = lax.axis_index("seq")
    output, input_grad, red_in, red_out, red_gate, red_up, red_down, red_small = step(
        w_in, w_out, w_gate, w_up, w_down, norm_gains, conv_taps, inputs, cotangent.reshape(ROWS, D)
    )
    red_small = lax.dynamic_slice(red_small, (0, seq * 8), (8, 8))
    red_gains, red_taps = red_small[:2], red_small[2:5]

    new = (
        adamw(norm_gains, red_gains, first_gains, second_gains, rate_small, 0.0),
        adamw(conv_taps, red_taps, first_taps, second_taps, rate_small, 0.0),
        adamw(w_in, red_in, first_in, second_in, rate_matrix, weight_decay),
        adamw(w_out, red_out, first_out, second_out, rate_matrix, weight_decay),
        adamw(w_gate, red_gate, first_gate, second_gate, rate_matrix, weight_decay),
        adamw(w_up, red_up, first_up, second_up, rate_matrix, weight_decay),
        adamw(w_down, red_down, first_down, second_down, rate_matrix, weight_decay),
    )
    return (
        output,
        input_grad,
        *[group[0] for group in new],
        *[group[1] for group in new],
        *[group[2] for group in new],
    )


def solution(mesh):
    tokens, columns, rows = P("dp", "seq", None), P(None, ("dp", "seq")), P(("dp", "seq"), None)
    weights = (columns, columns, rows, rows, rows, rows, rows)
    return jax.shard_map(
        shards,
        mesh=mesh,
        in_specs=(tokens, tokens) + weights * 3,
        out_specs=(tokens, tokens) + weights * 3,
        check_vma=False,
    )
```

time: 1740 us -> 185 us (0.11)
  waiting for transfers between devices: 1030 us -> 0 us
  blocking collectives: 500 us -> 0 us
  Pallas kernels: 0 us -> 174 us
  matrix products: 96 us -> 0 us
  starting transfers between devices: 40.9 us -> 0 us
  local copies, waits for them, and re-layouts: 27.4 us -> 3.21 us
  other arithmetic: 26.1 us -> 7.32 us
    reduce_scatter x4 -> x0, waiting for transfers between devices: 789 us -> none  [the longest x1 239 us: shards(): lax.psum_scatter(gate_weight_gradient, ('dp', 'seq'), scatter_dimension=0...]
    unnamed x2 -> x0, blocking collectives: 433 us -> none
    all_gather x5 -> x0, waiting for transfers between devices: 240 us -> none  [the longest x1 70.2 us: shards(): lax.all_gather(down_weight_reduced, ('dp', 'seq'), axis=0, tiled=True)]
    pallas_call x0 -> x1, Pallas kernels: none -> 174 us  [step(): pl.pallas_call(step_kernel, out_shape=tuple((jax.ShapeDtypeStruct(*shape)...]
    dot_general x15 -> x0, matrix products: 96 us -> none  [the longest x1 10.8 us: shards(): jnp.einsum('wzj,jg->wzg', normalized_second, gate_weight_float, preferred...]
    all_gather x2 -> x0, blocking collectives: 67.3 us -> none  [the longest x1 34.4 us: shards(): lax.all_gather(gains_low, ('dp', 'seq'), axis=1, tiled=True)]
    unnamed x13 -> x0, starting transfers between devices: 35.4 us -> none
    unnamed x77 -> x52, local copies, waits for them, and re-layouts: 26.7 us -> 3.14 us
  transfers between devices with their start and end apart: 24 -> 0, of which waited for: 12 -> 0; matrix products, arithmetic and copies ran while one was open for 28% -> 0% of each run, Pallas kernels for 0% -> 0%
where the time goes in v1:
time: 185 us
  Pallas kernels  174 us (94%)
  other arithmetic  7.32 us (4%)
  local copies, waits for them, and re-layouts  3.21 us (2%)
    pallas_call x1, Pallas kernels, step(): pl.pallas_call(step_kernel, out_shape=tuple((jax.ShapeDtypeStruct(*shape)...  174 us
    sub x6, other arithmetic, adamw(): weight - rate * (first_hat / (jnp.sqrt(second_hat) + epsilon_adam) + deca...  7.32 us

profile of v1, /device:TPU:1, one launch (start us, length us, event | category | flops | bytes accessed | tf_op | source)
XLA Modules:
  0.0 185.1 jit_solution(6039873854707258495)
XLA Ops:
  0.7 0.0 copy-start.5
  0.7 0.0 copy-start.14
  0.7 0.0 copy-start.15
  0.7 0.0 copy-start.17
  0.7 173.6 %step.1 = (bf16[2,128,1024]{2,1,0:T(8,128)(2,1)}, f32[2,128,1024]{2,1,0:T(8,128)}, f32[8,3072]{1,0:T(8,128)}, f32[8,1024]{1,0:T(8,128)}, f32[8,4608]{1,0:T(8,128...) custom-call(f32[8,3072]{1,0:T(8,128)} %refs_0_.1, f32[8,1024]{1,0:T(8,128)} %refs_1_.1, ...), custom_call_target="tpu_custom_call" | custom-call | tf_op jit(solution)/shard_map/step/pallas_call | solution.py:1079
  174.3 0.0 copy-start.19
  174.4 0.0 copy-start.18
  174.4 0.0 copy-start.21
  174.4 0.0 copy-start.22
  174.4 0.6 copy-done.19
  175.0 0.0 copy-start.20
  175.0 0.0 copy-start.23
  175.0 0.0 copy-start.24
  175.0 0.1 constant_dynamic-slice_fusion
  175.1 0.6 copy-done.20
  175.7 0.0 copy-done.23
  175.7 0.0 copy-done.24
  175.7 0.0 copy-start.13
  175.7 0.0 copy-start.16
  175.7 0.6 multiply_subtract_fusion.6
  176.3 0.0 copy-done.18
  176.3 0.0 copy-done.21
  176.3 0.0 copy-done.22
  176.3 0.6 multiply_subtract_fusion.5
  176.9 0.0 copy-done.5
  176.9 0.0 copy-done.14
  176.9 0.0 copy-done.15
  177.0 0.0 copy-start.3
  177.0 0.0 copy-start.9
  177.0 0.0 copy-start.10
  177.0 0.0 copy-start.11
  177.0 0.0 copy-start.12
  177.0 1.7 multiply_subtract_fusion.3
  178.7 0.0 copy-start.2
  178.7 0.0 copy-done.17
  178.7 0.0 copy-done.13
  178.7 0.0 copy-done.16
  178.8 1.4 multiply_subtract_fusion.4
  180.2 0.0 copy-done.3
  180.2 0.0 copy-done.9
  180.2 0.0 copy-done.10
  180.2 0.0 copy-done.11
  180.2 0.0 copy-done.12
  180.2 0.0 copy-done.2
  180.2 0.0 copy-start.1
  180.3 0.0 copy-start.6
  180.3 0.0 copy-start.7
  180.3 0.0 copy-start.8
  180.3 0.0 copy-start.4
  180.3 2.1 %multiply_subtract_fusion.1 = (f32[8,4608]{1,0:T(8,128)}, f32[8,4608]{1,0:T(8,128)}, f32[8,4608]{1,0:T(8,128)}, f32[8,4608]{1,0:T(8,128)}, f32[8,4608]{1,0:T(8,128)}, /*index=5*/f32[8,4608]{1,0:T(8,128)}) fusion(f32[8,4608]{1,0:T(8,128)S(1)} %copy-done.3, f32[8,4608]{1,0:T(8,128)} %get-tuple-element.37, f32[8,4608]{1,0:T(8,128)S(1)} %copy-done.9, ...), kind=kLoop, calls=%fused_computation.9 | loop fusion | flops 1105920 | bytes 2064384 | tf_op jit(solution)/shard_map/sub | solution.py:1104
  182.4 0.0 copy-done.1
  182.4 0.0 copy-done.6
  182.4 0.0 copy-done.7
  182.4 0.0 copy-done.8
  182.4 0.0 copy-start
  182.4 0.8 multiply_subtract_fusion
  183.3 0.0 copy-done.4
  183.3 0.8 copy.48
  184.1 0.0 copy-done
  184.1 1.0 copy.49
Async XLA Ops:
  0.7 176.3 %copy-start.5 = (f32[8,3072]{1,0:T(8,128)S(1)}, f32[8,3072]{1,0:T(8,128)}, u32[]{:S(2)}) copy-start(f32[8,3072]{1,0:T(8,128)} %refs_0_.1) | copy-start | bytes 294916
  0.7 176.3 %copy-start.14 = (f32[8,3072]{1,0:T(8,128)S(1)}, f32[8,3072]{1,0:T(8,128)}, u32[]{:S(2)}) copy-start(f32[8,3072]{1,0:T(8,128)} %param.34) | copy-start | bytes 294916
  0.7 176.3 %copy-start.15 = (f32[8,3072]{1,0:T(8,128)S(1)}, f32[8,3072]{1,0:T(8,128)}, u32[]{:S(2)}) copy-start(f32[8,3072]{1,0:T(8,128)} %param.41) | copy-start | bytes 294916
  0.7 178.1 %copy-start.17 = (f32[8,1024]{1,0:T(8,128)S(1)}, f32[8,1024]{1,0:T(8,128)}, u32[]{:S(2)}) copy-start(f32[8,1024]{1,0:T(8,128)} %param.42) | copy-start | bytes 98308
  174.3 0.7 copy-start.19
  174.4 2.0 %copy-start.18 = (f32[3,8]{1,0:T(4,128)S(1)}, f32[3,8]{1,0:T(4,128)}, u32[]{:S(2)}) copy-start(f32[3,8]{1,0:T(4,128)} %refs_6_.1) | copy-start | bytes 292
  174.4 2.0 %copy-start.21 = (f32[3,8]{1,0:T(4,128)S(1)}, f32[3,8]{1,0:T(4,128)}, u32[]{:S(2)}) copy-start(f32[3,8]{1,0:T(4,128)} %param.33) | copy-start | bytes 292
  174.4 2.0 %copy-start.22 = (f32[3,8]{1,0:T(4,128)S(1)}, f32[3,8]{1,0:T(4,128)}, u32[]{:S(2)}) copy-start(f32[3,8]{1,0:T(4,128)} %param.40) | copy-start | bytes 292
  175.0 0.7 copy-start.20
  175.0 0.7 copy-start.23
  175.0 0.7 copy-start.24
  175.7 3.0 %copy-start.13 = (f32[8,1024]{1,0:T(8,128)S(1)}, f32[8,1024]{1,0:T(8,128)}, u32[]{:S(2)}) copy-start(f32[8,1024]{1,0:T(8,128)} %refs_1_.1) | copy-start | bytes 98308
  175.7 3.0 %copy-start.16 = (f32[8,1024]{1,0:T(8,128)S(1)}, f32[8,1024]{1,0:T(8,128)}, u32[]{:S(2)}) copy-start(f32[8,1024]{1,0:T(8,128)} %param.35) | copy-start | bytes 98308
  177.0 3.2 %copy-start.3 = (f32[8,4608]{1,0:T(8,128)S(1)}, f32[8,4608]{1,0:T(8,128)}, u32[]{:S(2)}) copy-start(f32[8,4608]{1,0:T(8,128)} %refs_3_.1) | copy-start | bytes 442372
  177.0 3.2 %copy-start.9 = (f32[8,4608]{1,0:T(8,128)S(1)}, f32[8,4608]{1,0:T(8,128)}, u32[]{:S(2)}) copy-start(f32[8,4608]{1,0:T(8,128)} %param.37) | copy-start | bytes 442372
  177.0 3.2 %copy-start.10 = (f32[8,4608]{1,0:T(8,128)S(1)}, f32[8,4608]{1,0:T(8,128)}, u32[]{:S(2)}) copy-start(f32[8,4608]{1,0:T(8,128)} %param.44) | copy-start | bytes 442372
  177.0 3.2 %copy-start.11 = (f32[8,4608]{1,0:T(8,128)S(1)}, f32[8,4608]{1,0:T(8,128)}, u32[]{:S(2)}) copy-start(f32[8,4608]{1,0:T(8,128)} %param.43) | copy-start | bytes 442372
  177.0 3.2 %copy-start.12 = (f32[8,4608]{1,0:T(8,128)S(1)}, f32[8,4608]{1,0:T(8,128)}, u32[]{:S(2)}) copy-start(f32[8,4608]{1,0:T(8,128)} %param.36) | copy-start | bytes 442372
  178.7 1.5 copy-start.2
  180.2 2.2 %copy-start.1 = (f32[36,1024]{1,0:T(8,128)S(1)}, f32[36,1024]{1,0:T(8,128)}, u32[]{:S(2)}) copy-start(f32[36,1024]{1,0:T(8,128)} %refs_4_.1) | copy-start | bytes 442372
  180.3 2.2 %copy-start.6 = (f32[36,1024]{1,0:T(8,128)S(1)}, f32[36,1024]{1,0:T(8,128)}, u32[]{:S(2)}) copy-start(f32[36,1024]{1,0:T(8,128)} %param.38) | copy-start | bytes 442372
  180.3 2.2 %copy-start.7 = (f32[36,1024]{1,0:T(8,128)S(1)}, f32[36,1024]{1,0:T(8,128)}, u32[]{:S(2)}) copy-start(f32[36,1024]{1,0:T(8,128)} %param.45) | copy-start | bytes 442372
  180.3 2.1 %copy-start.8 = (f32[36,1024]{1,0:T(8,128)S(1)}, f32[36,1024]{1,0:T(8,128)}, u32[]{:S(2)}) copy-start(f32[36,1024]{1,0:T(8,128)} %get-tuple-element.38) | copy-start | bytes 442372
  180.3 3.0 %copy-start.4 = (bf16[2,128,1024]{2,1,0:T(8,128)(2,1)S(1)}, bf16[2,128,1024]{2,1,0:T(8,128)(2,1)}, u32[]{:S(2)}) copy-start(bf16[2,128,1024]{2,1,0:T(8,128)(2,1)} %get-tuple-element.86) | copy-start | bytes 1572868
  182.4 1.7 copy-start

commit v2 on v1

--- a/solution.py
+++ b/solution.py
@@ -225,6 +225,14 @@
     start, size = (32 * which, 32) if part is None else (32 * which + 16 * part, 16)
     lead = [slice(None)] * (len(ref.shape) - 2)
     return ref.at[(*lead, pl.ds(start, size), slice(None))]
+
+
+def rows_of(lanes):
+    def halves(ref, which, part):
+        rows = by_rows(ref, which, part)
+        return rows.at[(*[slice(None)] * (len(rows.shape) - 1), lanes)]
+
+    return halves
 
 
 def by_columns(ref, which, part):
@@ -279,6 +287,14 @@
         self.all_y.finish()
         self.all_x.finish()
 
+    def wait_near(self, then):
+        self.all_y.wait_below()
+        self.all_x.wait_below()
+        then(self, -1)
+        self.all_y.wait_above()
+        self.all_x.wait_above()
+        then(self, 1)
+
     def copies(self):
         return [copy for ring in (self.row_x, self.row_y, self.all_y, self.all_x) for copy in ring.copies_made()]
 
@@ -289,7 +305,16 @@
         return self.halves(self.view(everything, wrap(self.x + step)), 1, None)
 
 
-ORDERS = (("x", "y", "z"), ("y", "z", "x"), ("z", "x", "y"))
+PARTS = (
+    (0, pl.ds(0, 512), 0, ("y", "z", "x")),
+    (0, pl.ds(512, 512), 512, ("x", "y", "z")),
+    (1, pl.ds(0, 512), 1024, ("z", "x", "y")),
+    (1, pl.ds(512, 512), 1536, ("y", "z", "x")),
+)
+
+
+def first_half(width):
+    return (width + 255) // 256 * 128
 
 
 def cube_spots(spot, order):
@@ -312,7 +337,7 @@
     one, two, three = order
     everything = slice(None)
     place_of = {"y": 0, "x": 1, "z": 2}
-    first = make(a, to_a, lambda i: view(ref, **{one: i}), halver(-1, ref.shape[-1] // 2))
+    first = make(a, to_a, lambda i: view(ref, **{one: i}), halver(-1, first_half(ref.shape[-1])))
     second = make(b, to_b, lambda i: view(ref, **{one: everything, two: i}), halver(0, 2))
     third = make(
         c, to_c,
@@ -397,16 +422,22 @@
     return fed, downs
 
 
-def cube_landings(ref, order):
-    width = ref.shape[-1]
+def cube_landings(ref, lanes, order):
+    width, total = lanes.size, ref.shape[-1]
     place_of = {"y": 0, "x": 1, "z": 2}
     halved = (2, 4) if place_of[order[1]] < place_of[order[0]] else (4, 2)
-    single, half = ref.reshape(64, 16, width), pl.ds(0, width // 2)
-    first = [single.at[60, :, half], single.at[61, :, half], single.at[62], single.at[63]]
-    pairs, fours = ref.reshape(32, 2, 16, width), ref.reshape(16, 4, 16, width)
-    second = [pairs.at[24], pairs.at[25], fours.at[13], fours.at[14]]
-    lows, wholes = ref.reshape(8, *halved, 16, width), ref.reshape(4, 4, 4, 16, width)
-    third = [lows.at[4], lows.at[5], wholes.at[0], wholes.at[1]]
+
+    def take(count, lead, index, part=None):
+        window = lanes
+        if part is not None:
+            low = first_half(width)
+            window = pl.ds(lanes.start, low) if part == 0 else pl.ds(lanes.start, width - low)
+        places = (slice(None),) * (len(lead) + 1)
+        return ref.reshape(count, *lead, 16, total).at[(index, *places, window)]
+
+    first = [take(64, (), 60, 0), take(64, (), 61, 1), take(64, (), 62), take(64, (), 63)]
+    second = [take(32, (2,), 24), take(32, (2,), 25), take(16, (4,), 13), take(16, (4,), 14)]
+    third = [take(8, halved, 4), take(8, halved, 5), take(4, (4, 4), 0), take(4, (4, 4), 1)]
     return first, second, third
 
 
@@ -502,7 +533,7 @@
     "small_two": ((8, 128), F32),
     "g_small": ((8, 128), F32),
 }
-COPIES = 352
+COPIES = 448
 
 
 def step_kernel(*refs):
@@ -551,6 +582,20 @@
         other = wrap(seq + k + 1, PEERS)
         mix_copies.append(copies.start(m.mix_send.at[lax.rem(other, 2)], m.mix_got.at[seq], peer))
     m.mix_got[seq] = m.mix_send[core]
+    mixed, mixed_out = (
+        PlaneGather(copies, spot, lambda i, j: m.mix.at[core, i, j], rows_of(lanes), m.mix_block, halver(-2, 16))
+        for lanes in (pl.ds(HALF, 1536), pl.ds(0, HALF))
+    )
+    fed = PlaneGather(copies, spot, lambda i, j: m.feed.at[i, j], by_rows, m.feed_block, halver(-2, 16))
+    downs = PlaneGather(copies, spot, lambda i, j: m.down.at[i, j], by_columns, m.down_block, halver(-1, 640))
+    loads["w_down"].wait()
+    for i in range(4):
+        m.narrow_wide[4 * i : 4 * i + 4, 0:256] = m.w_down[32:36, 256 * i : 256 * i + 256]
+    m.down_block[:, 0:1024] = m.w_down[0:16, :].astype(BF)
+    m.down_block[:, 1024:2048] = m.w_down[16:32, :].astype(BF)
+    m.down_block[:, 2048:PACKED] = m.narrow_wide[0:16, 0:256].astype(BF)
+    m.down[y, x] = m.down_block[...]
+    downs.one()
     m.tile[...] = jnp.zeros_like(m.tile)
     m.tile[0:2, 0:8] = given.gains[...].astype(BF).astype(F32)
     m.tile[2:5, 0:8] = given.taps[...].astype(BF).astype(F32)
@@ -559,9 +604,6 @@
     edge_copy = copies.start(
         given.inputs.at[:, pl.ds(112, 16)], m.edge_in, (y * SIDE + x, wrap(seq + 1, PEERS))
     )
-    mixed = PlaneGather(copies, spot, lambda i, j: m.mix.at[core, i, j], by_rows, m.mix_block, halver(-2, 16))
-    fed = PlaneGather(copies, spot, lambda i, j: m.feed.at[i, j], by_rows, m.feed_block, halver(-2, 16))
-    downs = PlaneGather(copies, spot, lambda i, j: m.down.at[i, j], by_columns, m.down_block, halver(-1, 640))
     ring = RingGather(
         copies, z, to_z,
         lambda i: m.grads.at[i, core],
@@ -569,6 +611,24 @@
     )
     ring.plan(given.cotangent)
 
+    def slices(which):
+        for s in which:
+            gate = jnp.concatenate([m.w_gate[:, a : a + OWN] for a, _ in columns_of(s)], axis=1)
+            up = jnp.concatenate([m.w_up[:, a : a + OWN] for a, _ in columns_of(s)], axis=1)
+            tail = jnp.concatenate([gate[:, WIDE:], up[:, WIDE:]], axis=1)
+            upper = jnp.concatenate([gate[:, :WIDE], up[:, :128]], axis=1)
+            lower = jnp.concatenate([up[:, 128:WIDE], tail, jnp.zeros((8, 128), F32)], axis=1)
+            m.feed_send[s] = jnp.concatenate([upper, lower], axis=0).astype(BF)
+
+    loads["w_gate"].wait()
+    loads["w_up"].wait()
+    slices(range(PEERS))
+    feed_copies = []
+    for k, peer in enumerate(peers):
+        other = wrap(seq + k + 1, PEERS)
+        feed_copies.append(copies.start(m.feed_send.at[other], m.feed_got.at[seq], peer))
+    m.feed_got[seq] = m.feed_send[seq]
+    downs.two()
     for copy in mix_copies:
         copy.wait_recv()
     for k in range(4):
@@ -577,54 +637,10 @@
         m.mix_block[line, :1024] = jnp.concatenate([a[:8], b[:8]], axis=0).astype(BF)
         m.mix_block[line, 1024:] = jnp.concatenate([a[8:], b[8:]], axis=0).astype(BF)
     mixed.one()
+    mixed_out.one()
+    downs.three()
     m.mix[core, y, x] = m.mix_block[...]
-    ring.first()
-    cotangent_ring = ring
-    grads_passed = [copies.start(given.cotangent, m.grads.at[z, core], partner)]
-
-    def slices(which):
-        for s in which:
-            gate = jnp.concatenate([m.w_gate[:, a : a + OWN] for a, _ in columns_of(s)], axis=1)
-            up = jnp.concatenate([m.w_up[:, a : a + OWN] for a, _ in columns_of(s)], axis=1)
-            tail = jnp.concatenate([gate[:, WIDE:], up[:, WIDE:]], axis=1)
-            upper = jnp.concatenate([gate[:, :WIDE], up[:, :128]], axis=1)
-            lower = jnp.concatenate([up[:, 128:WIDE], tail, jnp.zeros((8, 128), F32)], axis=1)
-            m.feed_send[s] = jnp.concatenate([upper, lower], axis=0).astype(BF)
-
-    loads["w_gate"].wait()
-    loads["w_up"].wait()
-    slices(range(0, 4))
-    mixed.two()
-    slices(range(4, 8))
-    feed_copies = []
-    for k, peer in enumerate(peers):
-        other = wrap(seq + k + 1, PEERS)
-        feed_copies.append(copies.start(m.feed_send.at[other], m.feed_got.at[seq], peer))
-    m.feed_got[seq] = m.feed_send[seq]
-    for copy in small_copies:
-        copy.wait_recv()
-    m.small_send[...] = functools.reduce(lambda a, b: a + b, [m.small_got[s] for s in range(PEERS)])
-    small_x = [copies.start(m.small_send, m.small_all.at[y, x], device) for device in across]
-    m.small_all[y, x] = m.small_send[...]
-    mixed.three()
-    mix_passed = []
-
-    def pass_on(step):
-        for which in range(2):
-            part = mixed.group(which, step)
-            mix_passed.append(copies.start(part, part, partner))
-
-    pass_on(0)
-    for copy in small_x:
-        copy.wait_recv()
-    small_y = [copies.start(m.small_all.at[y], m.small_all.at[y], device) for device in along]
-    loads["w_down"].wait()
-    for i in range(4):
-        m.narrow_wide[4 * i : 4 * i + 4, 0:256] = m.w_down[32:36, 256 * i : 256 * i + 256]
-    m.down_block[:, 0:1024] = m.w_down[0:16, :].astype(BF)
-    m.down_block[:, 1024:2048] = m.w_down[16:32, :].astype(BF)
-    m.down_block[:, 2048:PACKED] = m.narrow_wide[0:16, 0:256].astype(BF)
-    m.down[y, x] = m.down_block[...]
+
     for copy in feed_copies:
         copy.wait_recv()
     for k in range(4):
@@ -633,6 +649,31 @@
         m.feed_block[line, :640] = jnp.concatenate([a[:8], b[:8]], axis=0).astype(BF)
         m.feed_block[line, 640:] = jnp.concatenate([a[8:, :512], b[8:, :512]], axis=0).astype(BF)
     m.feed[y, x] = m.feed_block[...]
+    fed.one()
+    ring.first()
+    cotangent_ring = ring
+    grads_passed = [copies.start(given.cotangent, m.grads.at[z, core], partner)]
+    mixed.two()
+    mixed_out.two()
+    for copy in small_copies:
+        copy.wait_recv()
+    m.small_send[...] = functools.reduce(lambda a, b: a + b, [m.small_got[s] for s in range(PEERS)])
+    small_x = [copies.start(m.small_send, m.small_all.at[y, x], device) for device in across]
+    m.small_all[y, x] = m.small_send[...]
+    mixed.three()
+    mix_passed = []
+
+    def pass_on(gather, step):
+        for which in range(2):
+            part = gather.group(which, step)
+            mix_passed.append(copies.start(part, part, partner))
+
+    pass_on(mixed, 0)
+    fed.two()
+    downs.four()
+    for copy in small_x:
+        copy.wait_recv()
+    small_y = [copies.start(m.small_all.at[y], m.small_all.at[y], device) for device in along]
     for copy in small_y:
         copy.wait_recv()
     m.rows[...] = small_rows(m.small_all)
@@ -645,29 +686,16 @@
     m.normed[ROWS:EVERY, :] = jnp.concatenate(earlier, axis=0).astype(BF)
     ring.second()
     mixed.four()
-    downs.one()
-    fed.one()
-    mixed.all_y.wait_below()
-    mixed.all_x.wait_below()
-    pass_on(-1)
-    mixed.all_y.wait_above()
-    mixed.all_x.wait_above()
-    pass_on(1)
-    downs.two()
-    fed.two()
-    downs.three()
-    fed.three()
+    mixed_out.three()
+    mixed.wait_near(pass_on)
     mixed.all_y.wait_far()
     mixed.all_x.wait_far()
-    pass_on(2)
-    ring.finish()
-    for step in (1, 3, 2):
-        chunk = m.grads.at[wrap(z + step), core]
-        grads_passed.append(copies.start(chunk, chunk, partner))
-
+    pass_on(mixed, 2)
+    mixed_out.four()
+    fed.three()
     for turn in range(2):
         if turn == 1:
-            for copy in mix_passed:
+            for copy in mix_passed[:8]:
                 copy.wait_recv()
         half = core if turn == 0 else 1 - core
         m.projected[half] = dot(m.normed[...], m.mix.at[half].reshape(D, 2048)[:, HALF:])
@@ -677,6 +705,13 @@
             extend(m.extended, m.projected, half, q)
             convolved = convolve(m.extended, m.rows[2:5, lanes])
             m.mixer_in[main, lanes] = (m.projected[half, main, HALF:1024] * convolved).astype(BF)
+    pass_on(mixed_out, 0)
+    mixed_out.wait_near(pass_on)
+    mixed_out.all_y.wait_far()
+    mixed_out.all_x.wait_far()
+    pass_on(mixed_out, 2)
+    for copy in mix_passed[8:]:
+        copy.wait_recv()
     weights = [m.mix.at[half].reshape(D, 2048) for half in range(2)]
     for half in range(2):
         lanes = slice(HALF * half, HALF * half + HALF)
@@ -699,8 +734,11 @@
     around.first()
     passed[0].start()
     m.tokens[z, core] = m.normed_two[...]
-    downs.four()
     fed.four()
+    ring.finish()
+    for step in (1, 3, 2):
+        chunk = m.grads.at[wrap(z + step), core]
+        grads_passed.append(copies.start(chunk, chunk, partner))
     gives, gives_left, gives_right = [], [], []
     for k in range(SIDE):
         theirs = m.part_out.at[k, 1 - core]
@@ -728,12 +766,6 @@
     loads["cotangent"].wait()
     fed.finish()
     feed = m.feed.reshape(D, 2 * SLICE)
-    around.second()
-    around.wait_above()
-    passed[1].start()
-    around.wait_below()
-    passed[2].start()
-
     @pl.loop(0, SIDE)
     def _(k):
         @pl.when(k == 0)
@@ -742,6 +774,11 @@
 
         @pl.when(k == 1)
         def _():
+            around.second()
+            around.wait_above()
+            passed[1].start()
+            around.wait_below()
+            passed[2].start()
             passed[1].wait_recv()
 
         @pl.when(k == 2)
@@ -861,21 +898,21 @@
         pl.semaphore_signal(ready.at[1], inc=1, device_id=device, device_id_type=MESH)
 
     sum_blocks = m.grads.reshape(2, 4, 4, 4, 16, D)
-    sum_views = [sum_blocks.at[0]] + [sum_blocks.at[1, :, :, :, :, pl.ds(HALF * k, HALF)] for k in range(2)]
 
     def flat_views(ref):
-        flat = ref.reshape(2, D, D)
-        return [flat.at[0], flat.at[1, :, pl.ds(0, HALF)], flat.at[1, :, pl.ds(HALF, HALF)]]
+        return [ref.reshape(2, D, D).at[group, :, lanes] for group, lanes, _, _ in PARTS]
 
     sum_flat, give_flat, got_flat = flat_views(m.grads), flat_views(m.tokens), flat_views(m.part)
     cubes = []
-    for ref, buffer, order in zip(sum_views, (m.landing, m.landing_left, m.landing_right), ORDERS):
-        lands = iter(cube_landings(buffer, order))
+    buffers = (m.landing, m.landing, m.landing_left, m.landing_right)
+    for (group, lanes, _, order), buffer in zip(PARTS, buffers):
+        room = lanes if buffer is m.landing else pl.ds(0, lanes.size)
+        lands = iter(cube_landings(buffer, room, order))
 
         def make(me, to, block, split, lands=lands):
             return RingReduce(copies, me, to, block, split, next(lands))
 
-        cubes.append(cube_rings(spot, order, ref, make))
+        cubes.append(cube_rings(spot, order, sum_blocks.at[group, :, :, :, :, lanes], make))
     save = local_copies(save_sem)
     saves = []
 
@@ -897,6 +934,36 @@
         grad_hidden[line, :] = total
         narrow[line, :] = total.astype(BF)
 
+    before = m.normed.at[0:ROWS]
+    grad_bc = m.grad_value.reshape(8, ROWS, 2 * SLICE)
+    given_parts = {}
+
+    def gradient(part, give):
+        half = 1 - core if give else core
+        target = (give_flat if give else sum_flat)[part]
+        left = m.mixer_in if part == 0 else before
+        right = (
+            lambda: narrow[:, half_lanes(half)],
+            lambda: grad_bc[6 + half, :, 0:HALF],
+            lambda: grad_bc[6 + half, :, HALF:D],
+            lambda: m.grad_x[half],
+        )[part]
+
+        @pl.loop(0, 4)
+        def _(n):
+            columns = pl.ds(pl.multiple_of(n * 256, 256), 256)
+            target[columns, :] = dot(left[:, columns], right(), TN).astype(BF)
+
+        if give:
+            given_parts[part] = copies.start(target, got_flat[part], partner)
+
+    def pass_to_cube(part):
+        given_parts[part].wait_recv()
+        accumulate(sum_flat[part], sum_flat[part], got_flat[part])
+        cubes[part][2].first()
+
+    pl.semaphore_wait(ready.at[1], len(neighbours))
+    gradient(0, True)
     grad_mixer[...] = dot(narrow[:, :HALF], weights[0][:, :HALF], NT) + dot(narrow[:, HALF:], weights[1][:, :HALF], NT)
     for q in range(2):
         for half in range(2):
@@ -904,8 +971,8 @@
             start = slice(128 * q, 128 * q + 8)
             m.edge_send[q, :, lanes] = grad_mixer[start, lanes] * m.projected[half, start, HALF:1024]
     edge_copy = copies.start(m.edge_send, m.edge_got, (y * SIDE + x, wrap(seq - 1, PEERS)))
+    gradient(0, False)
     fed.two()
-    grad_bc = m.grad_value.reshape(8, ROWS, 2 * SLICE)
     for half in range(2):
         lanes = slice(HALF * half, HALF * half + HALF)
         for q in range(2):
@@ -913,11 +980,9 @@
             extend(m.extended, m.projected, half, q)
             upstream = grad_mixer[main, lanes]
             grad_bc[6 + half, main, HALF:D] = (upstream * convolve(m.extended, m.rows[2:5, lanes])).astype(BF)
-            back = upstream * m.projected[half, main, HALF:1024]
-            m.grad_conv[q, 0:128, lanes] = back
-            for k in range(3):
-                m.sums[2 + k : 3 + k, lanes] += jnp.sum(back * m.extended[6 + k : 134 + k, :], axis=0, keepdims=True)
-    ring.second()
+            m.grad_conv[q, 0:128, lanes] = upstream * m.projected[half, main, HALF:1024]
+    gradient(2, True)
+    pass_to_cube(0)
     edge_copy.wait_recv()
     inside = (seq < PEERS - 1).astype(F32)
     for q in range(2):
@@ -933,31 +998,23 @@
             )
             grad_bc[6 + half, main, 0:HALF] = (gated * m.projected[half, main, 1024:]).astype(BF)
             m.grad_x[half, main, :] = (gated * m.projected[half, main, :HALF]).astype(BF)
+    gradient(1, True)
+    gradient(3, True)
+    gradient(2, False)
+    pass_to_cube(2)
     downs.two()
-
-    before = m.normed.at[0:ROWS]
-    given_parts = []
-    for targets, half in ((give_flat, 1 - core), (sum_flat, core)):
-        back, back_x, back_out = grad_bc.at[6 + half], m.grad_x.at[half], narrow.at[:, half_lanes(half)]
-
-        @pl.loop(0, 4)
-        def _(n, targets=targets, back=back, back_x=back_x, back_out=back_out):
-            columns = pl.ds(pl.multiple_of(n * 256, 256), 256)
-            left = before[:, columns]
-            first = dot(left, back[:, 0:D], TN).astype(BF)
-            targets[0][columns, HALF:D] = first[:, :HALF]
-            targets[1][columns, :] = first[:, HALF:]
-            targets[2][columns, :] = dot(left, back_x[...], TN).astype(BF)
-            targets[0][columns, 0:HALF] = dot(m.mixer_in[:, columns], back_out[...], TN).astype(BF)
-
-        if targets is give_flat:
-            pl.semaphore_wait(ready.at[1], len(neighbours))
-            for part in range(3):
-                given_parts.append(copies.start(give_flat[part], got_flat[part], partner))
-    for part in range(3):
-        given_parts[part].wait_recv()
-        accumulate(sum_flat[part], sum_flat[part], got_flat[part])
-        cubes[part][2].first()
+    ring.second()
+    gradient(1, False)
+    pass_to_cube(1)
+    gradient(3, False)
+    pass_to_cube(3)
+    for half in range(2):
+        lanes = slice(HALF * half, HALF * half + HALF)
+        for q in range(2):
+            extend(m.extended, m.projected, half, q)
+            back = m.grad_conv[q, 0:128, lanes]
+            for k in range(3):
+                m.sums[2 + k : 3 + k, lanes] += jnp.sum(back * m.extended[6 + k : 134 + k, :], axis=0, keepdims=True)
     fed.three()
     downs.three()
 
@@ -981,7 +1038,7 @@
     for q in range(2):
         saves.append(save(grad_mixer.at[128 * q : 128 * q + 128], result.input_grad.at[q]))
 
-    for part in range(3):
+    for part in (0, 2, 1, 3):
         cubes[part][2].second()
     fed.four()
     downs.four()
@@ -1003,7 +1060,7 @@
         copies.start(m.small_one.at[wrap(x + k)], m.small_x.at[k], device)
         for k, device in zip(range(1, SIDE), across)
     ]
-    for part in (1, 2, 0):
+    for part in (0, 2, 1, 3):
         cubes[part][2].finish()
         cubes[part][1].first()
     fed.finish(m.feed_wide)
@@ -1026,40 +1083,40 @@
     m.small_two[...] = total
     sent_z = [copies.start(m.small_two, m.small_z.at[seq], peer) for peer in peers]
     m.small_z[seq] = total
-    for part in (1, 2, 0):
+    for part in (0, 2, 1, 3):
         cubes[part][1].second()
+    for copy in sent_z:
+        copy.wait_recv()
+    m.g_small[...] = functools.reduce(lambda a, b: a + b, [m.small_z[s] for s in range(PEERS)])
+    saves.append(save(m.g_small, result.g_small))
+    for copy in sent_feed:
+        copy.wait_recv()
+    def spread(main, tail, target, output):
+        for d in range(16):
+            pieces = []
+            for s in range(PEERS):
+                line = m.feed_land[s]
+                whole = jnp.concatenate([line[:, main : main + WIDE], line[:, tail : tail + 64]], axis=1)
+                pieces.append(whole[:, OWN * d : OWN * d + OWN])
+            target[:, 288 * d : 288 * d + 288] = jnp.concatenate(pieces, axis=1)
+        saves.append(save(target, output))
+
+    for part in (0, 2, 1, 3):
+        cubes[part][1].finish()
+        cubes[part][0].first()
+    spread(0, 1024, m.w_gate, result.g_gate)
+    for part in (0, 2, 1, 3):
+        cubes[part][0].second()
+    spread(WIDE, 1088, m.w_up, result.g_up)
+    for part, (_, lanes, start, _) in enumerate(PARTS):
+        cubes[part][0].finish(m.mix_wide.at[:, pl.ds(start, lanes.size)])
+    theirs = pl.ds(pl.multiple_of((1 - core) * 8, 8), 8)
+    mix_copy = copies.start(m.mix_wide.at[theirs], m.mix_land.at[core], partner)
+    m.mix_land[core] = m.mix_wide[pl.ds(pl.multiple_of(core * 8, 8), 8), :]
     ring.finish(grad_hidden)
     m.mixer_in[...] = (m.hidden[...] + grad_hidden[...]).astype(BF)
     for q in range(2):
         saves.append(save(m.mixer_in.at[128 * q : 128 * q + 128], result.output.at[q]))
-    for copy in sent_feed:
-        copy.wait_recv()
-    for d in range(16):
-        gates, ups = [], []
-        for s in range(PEERS):
-            line = m.feed_land[s]
-            gate = jnp.concatenate([line[:, :WIDE], line[:, 1024:1088]], axis=1)
-            up = jnp.concatenate([line[:, WIDE:1024], line[:, 1088:1152]], axis=1)
-            gates.append(gate[:, OWN * d : OWN * d + OWN])
-            ups.append(up[:, OWN * d : OWN * d + OWN])
-        m.w_gate[:, 288 * d : 288 * d + 288] = jnp.concatenate(gates, axis=1)
-        m.w_up[:, 288 * d : 288 * d + 288] = jnp.concatenate(ups, axis=1)
-    saves.append(save(m.w_gate, result.g_gate))
-    saves.append(save(m.w_up, result.g_up))
-    for copy in sent_z:
-        copy.wait_recv()
-    m.g_small[...] = functools.reduce(lambda a, b: a + b, [m.small_z[s] for s in range(PEERS)])
-    saves.append(save(m.g_small, result.g_small))
-    for part in (1, 2, 0):
-        cubes[part][1].finish()
-        cubes[part][0].first()
-    for part in range(3):
-        cubes[part][0].second()
-    for part, (start, size) in enumerate(((0, D), (D, HALF), (D + HALF, HALF))):
-        cubes[part][0].finish(m.mix_wide.at[:, pl.ds(start, size)])
-    theirs = pl.ds(pl.multiple_of((1 - core) * 8, 8), 8)
-    mix_copy = copies.start(m.mix_wide.at[theirs], m.mix_land.at[core], partner)
-    m.mix_land[core] = m.mix_wide[pl.ds(pl.multiple_of(core * 8, 8), 8), :]
     mix_copy.wait_recv()
     for half in range(2):
         for k in range(3):
@@ -1096,6 +1153,11 @@
     )(*operands)
 
 
+SHAPES = ((2, 8), (3, 8), (8, 3072), (8, 1024), (8, 4608), (8, 4608), (OWN, D))
+RATES = ((rate_small, 0.0),) * 2 + ((rate_matrix, weight_decay),) * 5
+TILED = 5
+
+
 def adamw(weight, grad, first, second, rate, decay):
     first_new = beta_one * first + (1.0 - beta_one) * grad
     second_new = beta_two * second + (1.0 - beta_two) * grad * grad
@@ -1107,34 +1169,78 @@
     return (weight_new, first_new, second_new)
 
 
+def adamw_kernel(*refs):
+    weights, firsts, seconds, refs = refs[:7], refs[7:14], refs[14:21], refs[21:]
+    small_grad, grads, finished, refs = refs[0], refs[1:6], refs[6:8], refs[8:]
+    outs, final, refs = (refs[:7], refs[7:14], refs[14:21]), refs[21:23], refs[23:]
+    held = [refs[5 * k : 5 * k + 5] for k in range(4)]
+    through, (load_sem, save_sem) = refs[20:22], refs[22:]
+    load, save = local_copies(load_sem), local_copies(save_sem)
+    passing = [load(source, kept) for source, kept in zip(finished, through)]
+    loads = []
+    for index in range(TILED):
+        sources = (grads[index], weights[index + 2], firsts[index + 2], seconds[index + 2])
+        loads.append([load(source, kept[index]) for source, kept in zip(sources, held)])
+    seq = lax.axis_index("seq")
+    tile = pltpu.roll(small_grad[...], lax.rem(128 - seq * 8, 128), 1)
+    for index, (start, count) in enumerate(((0, 2), (2, 3))):
+        grad = tile[start : start + count, 0:8]
+        new = adamw(weights[index][...], grad, firsts[index][...], seconds[index][...], *RATES[index])
+        for out, value in zip(outs, new):
+            out[index][...] = value
+    saves = []
+    for copy, kept, target in zip(passing, through, final):
+        copy.wait()
+        saves.append(save(kept, target))
+    for index in range(TILED):
+        for copy in loads[index]:
+            copy.wait()
+        grad, weight, first, second = (kept[index] for kept in held)
+        rows, columns = weight.shape
+        for start in range(0, columns, 512):
+            lanes = slice(start, min(start + 512, columns))
+            new = adamw(weight[:, lanes], grad[:, lanes], first[:, lanes], second[:, lanes], *RATES[index + 2])
+            weight[:, lanes], first[:, lanes], second[:, lanes] = new
+        for out, kept in zip(outs, (weight, first, second)):
+            saves.append(save(kept, out[index + 2]))
+    for copy in saves:
+        copy.wait()
+
+
+def adamw_all(weights, firsts, seconds, small_grad, grads, finished):
+    hbm, vmem = pl.BlockSpec(memory_space=pl.ANY), pl.BlockSpec(memory_space=pltpu.VMEM)
+    group = [vmem] * 2 + [hbm] * TILED
+    return pl.pallas_call(
+        adamw_kernel,
+        out_shape=[jax.ShapeDtypeStruct(shape, F32) for shape in SHAPES] * 3
+        + [jax.ShapeDtypeStruct(array.shape, array.dtype) for array in finished],
+        in_specs=group * 3 + [vmem] + [hbm] * (TILED + 2),
+        out_specs=group * 3 + [hbm] * 2,
+        scratch_shapes=[pltpu.VMEM(shape, F32) for shape in SHAPES[2:]] * 4
+        + [pltpu.VMEM(array.shape, array.dtype) for array in finished]
+        + [pltpu.SemaphoreType.DMA((4 * TILED + 2,)), pltpu.SemaphoreType.DMA((3 * TILED + 2,))],
+        compiler_params=pltpu.CompilerParams(vmem_limit_bytes=VMEM_BYTES),
+        name="adamw",
+    )(*weights, *firsts, *seconds, small_grad, *grads, *finished)
+
+
 def shards(
     inputs, cotangent, norm_gains, conv_taps, w_in, w_out, w_gate, w_up, w_down,
     first_gains, first_taps, first_in, first_out, first_gate, first_up, first_down,
     second_gains, second_taps, second_in, second_out, second_gate, second_up, second_down,
 ):
-    seq = lax.axis_index("seq")
     output, input_grad, red_in, red_out, red_gate, red_up, red_down, red_small = step(
         w_in, w_out, w_gate, w_up, w_down, norm_gains, conv_taps, inputs, cotangent.reshape(ROWS, D)
     )
-    red_small = lax.dynamic_slice(red_small, (0, seq * 8), (8, 8))
-    red_gains, red_taps = red_small[:2], red_small[2:5]
-
-    new = (
-        adamw(norm_gains, red_gains, first_gains, second_gains, rate_small, 0.0),
-        adamw(conv_taps, red_taps, first_taps, second_taps, rate_small, 0.0),
-        adamw(w_in, red_in, first_in, second_in, rate_matrix, weight_decay),
-        adamw(w_out, red_out, first_out, second_out, rate_matrix, weight_decay),
-        adamw(w_gate, red_gate, first_gate, second_gate, rate_matrix, weight_decay),
-        adamw(w_up, red_up, first_up, second_up, rate_matrix, weight_decay),
-        adamw(w_down, red_down, first_down, second_down, rate_matrix, weight_decay),
+    *new, output, input_grad = adamw_all(
+        (norm_gains, conv_taps, w_in, w_out, w_gate, w_up, w_down),
+        (first_gains, first_taps, first_in, first_out, first_gate, first_up, first_down),
+        (second_gains, second_taps, second_in, second_out, second_gate, second_up, second_down),
+        red_small,
+        (red_in, red_out, red_gate, red_up, red_down),
+        (output, input_grad),
     )
-    return (
-        output,
-        input_grad,
-        *[group[0] for group in new],
-        *[group[1] for group in new],
-        *[group[2] for group in new],
-    )
+    return (output, input_grad, *new)
 
 
 def solution(mesh):

time: 185 us -> 172 us (0.930)
  other arithmetic: 7.32 us -> 0 us
  local copies, waits for them, and re-layouts: 3.21 us -> 0 us
  Pallas kernels: 174 us -> 171 us
    pallas_call x1, Pallas kernels: 174 us -> 166 us  [step(): pl.pallas_call(step_kernel, out_shape=tuple((jax.ShapeDtypeStruct(*shape)...]
    sub x6 -> x0, other arithmetic: 7.32 us -> none  [adamw(): weight - rate * (first_hat / (jnp.sqrt(second_hat) + epsilon_adam) + deca...]
    pallas_call x0 -> x1, Pallas kernels: none -> 5.03 us  [adamw_all(): pl.pallas_call(adamw_kernel, out_shape=[jax.ShapeDtypeStruct(shape, F32)...]
    unnamed x52 -> x0, local copies, waits for them, and re-layouts: 3.14 us -> none
where the time goes in v2:
time: 172 us
  Pallas kernels  171 us (99%)
    pallas_call x1, Pallas kernels, step(): pl.pallas_call(step_kernel, out_shape=tuple((jax.ShapeDtypeStruct(*shape)...  166 us
    pallas_call x1, Pallas kernels, adamw_all(): pl.pallas_call(adamw_kernel, out_shape=[jax.ShapeDtypeStruct(shape, F32)...  5.03 us

profile of v2, /device:TPU:1, one launch (start us, length us, event | category | flops | bytes accessed | tf_op | source)
XLA Modules:
  0.0 171.8 jit_solution(13738620119390822982)
XLA Ops:
  0.7 166.0 %step.1 = (bf16[2,128,1024]{2,1,0:T(8,128)(2,1)}, f32[2,128,1024]{2,1,0:T(8,128)}, f32[8,3072]{1,0:T(8,128)}, f32[8,1024]{1,0:T(8,128)}, f32[8,4608]{1,0:T(8,128...) custom-call(f32[8,3072]{1,0:T(8,128)} %refs_2_.3, f32[8,1024]{1,0:T(8,128)} %refs_3_.3, ...), custom_call_target="tpu_custom_call" | custom-call | tf_op jit(solution)/shard_map/step/pallas_call | solution.py:1136
  166.6 5.0 %adamw.1 = (f32[2,8]{1,0:T(2,128)}, f32[3,8]{1,0:T(4,128)}, f32[8,3072]{1,0:T(8,128)}, f32[8,1024]{1,0:T(8,128)}, f32[8,4608]{1,0:T(8,128)}, /*index=5*/f32[8,46...) custom-call(f32[2,8]{1,0:T(2,128)} %refs_0_.3, ...), custom_call_target="tpu_custom_call" | custom-call | tf_op jit(solution)/shard_map/adamw/pallas_call | solution.py:1213

commit v3 on v2

--- a/solution.py
+++ b/solution.py
@@ -90,8 +90,8 @@
 
 
 class RingGather:
-    def __init__(self, copies, me, to, block, split):
-        self.copies, self.me, self.to, self.block, self.split = copies, me, to, block, split
+    def __init__(self, copies, me, to, block, split, fine=True):
+        self.copies, self.me, self.to, self.block, self.split, self.fine = copies, me, to, block, split, fine
 
     def plan(self, source=None):
         source = self.block(self.me) if source is None else source
@@ -101,8 +101,12 @@
             return self.copies.plan(self.split(start, part), self.split(target, part), self.to(place))
 
         mine, before, after = self.block(self.me), self.block(below), self.block(above)
-        self.up = [move(source, mine, part, above) for part in range(2)]
-        self.down = [move(source, mine, part, below) for part in range(2)]
+        if self.fine:
+            self.up = [move(source, mine, part, above) for part in range(2)]
+            self.down = [move(source, mine, part, below) for part in range(2)]
+        else:
+            self.up = [self.copies.plan(source, mine, self.to(above))]
+            self.down = [self.copies.plan(source, mine, self.to(below))]
         self.pass_up = move(before, before, 0, above)
         self.pass_down = move(after, after, 1, below)
 
@@ -110,21 +114,24 @@
         if not hasattr(self, "up"):
             self.plan(source)
         self.up[0].start()
-        self.down[1].start()
-        self.up[1].start()
-        self.down[0].start()
+        self.down[-1].start()
+        if self.fine:
+            self.up[1].start()
+            self.down[0].start()
 
     def second(self):
         self.up[0].wait_recv()
         self.pass_up.start()
-        self.down[1].wait_recv()
+        self.down[-1].wait_recv()
         self.pass_down.start()
 
     def wait_below(self):
-        self.up[1].wait_recv()
+        if self.fine:
+            self.up[1].wait_recv()
 
     def wait_above(self):
-        self.down[0].wait_recv()
+        if self.fine:
+            self.down[0].wait_recv()
 
     def wait_far(self):
         self.pass_up.wait_recv()
@@ -140,8 +147,8 @@
 
 
 class RingReduce:
-    def __init__(self, copies, me, to, block, split, landing):
-        self.copies, self.me, self.to, self.block, self.split = copies, me, to, block, split
+    def __init__(self, copies, me, to, block, split, landing, fine=True):
+        self.copies, self.me, self.to, self.block, self.split, self.fine = copies, me, to, block, split, fine
         self.low_in, self.high_in, self.plus_in, self.minus_in = landing
 
     def plan(self):
@@ -149,8 +156,12 @@
         plan, split = self.copies.plan, self.split
         self.far_up = plan(split(self.block(far), 0), self.low_in, self.to(above))
         self.far_down = plan(split(self.block(far), 1), self.high_in, self.to(below))
-        self.up = [plan(split(self.block(above), k), split(self.plus_in, k), self.to(above)) for k in range(2)]
-        self.down = [plan(split(self.block(below), k), split(self.minus_in, k), self.to(below)) for k in range(2)]
+        if self.fine:
+            self.up = [plan(split(self.block(above), k), split(self.plus_in, k), self.to(above)) for k in range(2)]
+            self.down = [plan(split(self.block(below), k), split(self.minus_in, k), self.to(below)) for k in range(2)]
+        else:
+            self.up = [plan(self.block(above), self.plus_in, self.to(above))]
+            self.down = [plan(self.block(below), self.minus_in, self.to(below))]
 
     def first_far(self):
         self.far_up.start()
@@ -166,8 +177,9 @@
         if not hasattr(self, "up"):
             self.plan()
         self.first_far()
-        self.first_above()
-        self.first_below()
+        if self.fine:
+            self.first_above()
+            self.first_below()
 
     def second(self):
         below, above = self.block(wrap(self.me - 1)), self.block(wrap(self.me + 1))
@@ -176,7 +188,7 @@
         self.up[0].start()
         self.far_down.wait_recv()
         accumulate(self.split(below, 1), self.split(below, 1), self.high_in)
-        self.down[1].start()
+        self.down[-1].start()
 
     def copies_made(self):
         return [self.far_up, self.far_down, *self.up, *self.down]
@@ -251,15 +263,15 @@
 
 
 class PlaneGather:
-    def __init__(self, copies, spot, view, halves, block, split):
+    def __init__(self, copies, spot, view, halves, block, split, fine=True):
         x, y, z, core = spot
         to_x, to_y = (lambda i: at(i, y, z, core)), (lambda i: at(x, i, z, core))
         everything, fours = slice(None), halver(0, 2)
         self.x, self.y, self.view, self.halves = x, y, view, halves
-        self.row_x = RingGather(copies, x, to_x, lambda i: halves(view(y, i), 0, None), split)
-        self.row_y = RingGather(copies, y, to_y, lambda i: halves(view(i, x), 1, None), split)
-        self.all_y = RingGather(copies, y, to_y, lambda i: halves(view(i, everything), 0, None), fours)
-        self.all_x = RingGather(copies, x, to_x, lambda i: halves(view(everything, i), 1, None), fours)
+        self.row_x = RingGather(copies, x, to_x, lambda i: halves(view(y, i), 0, None), split, False)
+        self.row_y = RingGather(copies, y, to_y, lambda i: halves(view(i, x), 1, None), split, False)
+        self.all_y = RingGather(copies, y, to_y, lambda i: halves(view(i, everything), 0, None), fours, fine)
+        self.all_x = RingGather(copies, x, to_x, lambda i: halves(view(everything, i), 1, None), fours, fine)
         self.row_x.plan(halves(block, 0, None))
         self.row_y.plan(halves(block, 1, None))
         self.all_y.plan()
@@ -337,12 +349,13 @@
     one, two, three = order
     everything = slice(None)
     place_of = {"y": 0, "x": 1, "z": 2}
-    first = make(a, to_a, lambda i: view(ref, **{one: i}), halver(-1, first_half(ref.shape[-1])))
-    second = make(b, to_b, lambda i: view(ref, **{one: everything, two: i}), halver(0, 2))
+    first = make(a, to_a, lambda i: view(ref, **{one: i}), halver(-1, first_half(ref.shape[-1])), False)
+    second = make(b, to_b, lambda i: view(ref, **{one: everything, two: i}), halver(0, 2), False)
     third = make(
         c, to_c,
         lambda i: view(ref, **{one: everything, two: everything, three: i}),
         halver(0 if place_of[two] < place_of[one] else 1, 2),
+        True,
     )
     return first, second, third
 
@@ -380,8 +393,8 @@
         self.halves = halves
         self.all_y = RingReduce(copies, y, to_y, lambda i: halves(view(i, everything), 0, None), fours, landings[0:4])
         self.all_x = RingReduce(copies, x, to_x, lambda i: halves(view(everything, i), 1, None), fours, landings[4:8])
-        self.row_x = RingReduce(copies, x, to_x, lambda i: halves(view(y, i), 0, None), split, landings[8:12])
-        self.row_y = RingReduce(copies, y, to_y, lambda i: halves(view(i, x), 1, None), split, landings[12:16])
+        self.row_x = RingReduce(copies, x, to_x, lambda i: halves(view(y, i), 0, None), split, landings[8:12], False)
+        self.row_y = RingReduce(copies, y, to_y, lambda i: halves(view(i, x), 1, None), split, landings[12:16], False)
 
     def one(self):
         self.all_y.first()
@@ -587,7 +600,7 @@
         for lanes in (pl.ds(HALF, 1536), pl.ds(0, HALF))
     )
     fed = PlaneGather(copies, spot, lambda i, j: m.feed.at[i, j], by_rows, m.feed_block, halver(-2, 16))
-    downs = PlaneGather(copies, spot, lambda i, j: m.down.at[i, j], by_columns, m.down_block, halver(-1, 640))
+    downs = PlaneGather(copies, spot, lambda i, j: m.down.at[i, j], by_columns, m.down_block, halver(-1, 640), False)
     loads["w_down"].wait()
     for i in range(4):
         m.narrow_wide[4 * i : 4 * i + 4, 0:256] = m.w_down[32:36, 256 * i : 256 * i + 256]
@@ -766,6 +779,23 @@
     loads["cotangent"].wait()
     fed.finish()
     feed = m.feed.reshape(D, 2 * SLICE)
+
+    def settle(step):
+        gives[step].wait_recv()
+        accumulate(m.part.at[step, core], m.part.at[step, core], m.landing.at[step])
+        if step == 1:
+            reduce.first_above()
+        if step == 2:
+            reduce.first_below()
+        if step == 3:
+            reduce.first_far()
+
+    def output_part(step):
+        lines = pl.ds(pl.multiple_of(visit(z, step) * PAIR, PAIR), PAIR)
+        m.part_out.at[step].reshape(PAIR, D)[...] = dot(m.active[lines, :], m.down_rows[...]).astype(BF)
+        gives_left[step].start()
+        gives_right[step].start()
+
     @pl.loop(0, SIDE)
     def _(k):
         @pl.when(k == 0)
@@ -794,6 +824,11 @@
         chip = visit(z, k)
         m.value[...] = dot(m.tokens.at[chip].reshape(PAIR, D)[...], feed[...])
         m.grad_active[...] = dot(m.grads.at[chip].reshape(PAIR, D)[...], m.down_rows[...], NT)
+        for step in range(SIDE - 1):
+            @pl.when(k == step + 1)
+            def _(step=step):
+                settle(step)
+
         base = chip * PAIR
 
         @pl.loop(0, PAIR // 64)
@@ -823,21 +858,10 @@
             @pl.when(k == step)
             def _(step=step):
                 gives[step].start()
-        m.part_out.at[k].reshape(PAIR, D)[...] = dot(m.active[lines, :], m.down_rows[...]).astype(BF)
-        for step in range(SIDE):
-            @pl.when(k == step)
-            def _(step=step):
-                gives_left[step].start()
-                gives_right[step].start()
-                gives[step].wait_recv()
-                accumulate(m.part.at[step, core], m.part.at[step, core], m.landing.at[step])
-                if step == 1:
-                    reduce.first_above()
-                if step == 2:
-                    reduce.first_below()
-                if step == 3:
-                    reduce.first_far()
-
+
+    output_part(0)
+    output_part(1)
+    settle(3)
     copies.drain(fed.copies())
     copies.drain(downs.copies())
     every_grad, every_token = m.grads.reshape(2048, D), m.tokens.reshape(2048, D)
@@ -868,6 +892,8 @@
     down_columns(0)
     pl.semaphore_wait(ready.at[0], len(plane_neighbours))
     fed.one()
+    output_part(2)
+    output_part(3)
     for n in range(1, 4):
         down_columns(n)
     for d in range(16):
@@ -909,8 +935,8 @@
         room = lanes if buffer is m.landing else pl.ds(0, lanes.size)
         lands = iter(cube_landings(buffer, room, order))
 
-        def make(me, to, block, split, lands=lands):
-            return RingReduce(copies, me, to, block, split, next(lands))
+        def make(me, to, block, split, fine, lands=lands):
+            return RingReduce(copies, me, to, block, split, next(lands), fine)
 
         cubes.append(cube_rings(spot, order, sum_blocks.at[group, :, :, :, :, lanes], make))
     save = local_copies(save_sem)

time: 172 us -> 170 us (0.988)
  Pallas kernels: 171 us -> 169 us
where the time goes in v3:
time: 170 us
  Pallas kernels  169 us (99%)
    pallas_call x1, Pallas kernels, step(): pl.pallas_call(step_kernel, out_shape=tuple((jax.ShapeDtypeStruct(*shape)...  164 us
    pallas_call x1, Pallas kernels, adamw_all(): pl.pallas_call(adamw_kernel, out_shape=[jax.ShapeDtypeStruct(shape, F32)...  5.03 us

profile of v3, /device:TPU:1, one launch (start us, length us, event | category | flops | bytes accessed | tf_op | source)
XLA Modules:
  0.0 170.2 jit_solution(1661410411593569594)
XLA Ops:
  0.7 164.4 %step.1 = (bf16[2,128,1024]{2,1,0:T(8,128)(2,1)}, f32[2,128,1024]{2,1,0:T(8,128)}, f32[8,3072]{1,0:T(8,128)}, f32[8,1024]{1,0:T(8,128)}, f32[8,4608]{1,0:T(8,128...) custom-call(f32[8,3072]{1,0:T(8,128)} %refs_2_.3, f32[8,1024]{1,0:T(8,128)} %refs_3_.3, ...), custom_call_target="tpu_custom_call" | custom-call | tf_op jit(solution)/shard_map/step/pallas_call | solution.py:1162
  165.0 5.0 %adamw.1 = (f32[2,8]{1,0:T(2,128)}, f32[3,8]{1,0:T(4,128)}, f32[8,3072]{1,0:T(8,128)}, f32[8,1024]{1,0:T(8,128)}, f32[8,4608]{1,0:T(8,128)}, /*index=5*/f32[8,46...) custom-call(f32[2,8]{1,0:T(2,128)} %refs_0_.3, ...), custom_call_target="tpu_custom_call" | custom-call | tf_op jit(solution)/shard_map/adamw/pallas_call | solution.py:1239

commit v4 on v3

--- a/solution.py
+++ b/solution.py
@@ -653,6 +653,8 @@
     mixed_out.one()
     downs.three()
     m.mix[core, y, x] = m.mix_block[...]
+    mixed.two()
+    mixed_out.two()
 
     for copy in feed_copies:
         copy.wait_recv()
@@ -666,22 +668,20 @@
     ring.first()
     cotangent_ring = ring
     grads_passed = [copies.start(given.cotangent, m.grads.at[z, core], partner)]
-    mixed.two()
-    mixed_out.two()
+    mixed.three()
+    mix_passed = []
+
+    def pass_on(gather, step):
+        for which in range(2):
+            part = gather.group(which, step)
+            mix_passed.append(copies.start(part, part, partner))
+
+    pass_on(mixed, 0)
     for copy in small_copies:
         copy.wait_recv()
     m.small_send[...] = functools.reduce(lambda a, b: a + b, [m.small_got[s] for s in range(PEERS)])
     small_x = [copies.start(m.small_send, m.small_all.at[y, x], device) for device in across]
     m.small_all[y, x] = m.small_send[...]
-    mixed.three()
-    mix_passed = []
-
-    def pass_on(gather, step):
-        for which in range(2):
-            part = gather.group(which, step)
-            mix_passed.append(copies.start(part, part, partner))
-
-    pass_on(mixed, 0)
     fed.two()
     downs.four()
     for copy in small_x:

time: 170 us -> 170 us (level)
  no operation moved by 1% of the time
where the time goes in v4:
time: 170 us; the launch traced here: 169 us
  Pallas kernels  169 us (99%)
    pallas_call x1, Pallas kernels, step(): pl.pallas_call(step_kernel, out_shape=tuple((jax.ShapeDtypeStruct(*shape)...  164 us
    pallas_call x1, Pallas kernels, adamw_all(): pl.pallas_call(adamw_kernel, out_shape=[jax.ShapeDtypeStruct(shape, F32)...  5.03 us

profile of v4, /device:TPU:1, one launch (start us, length us, event | category | flops | bytes accessed | tf_op | source)
XLA Modules:
  0.0 169.5 jit_solution(10587087333670974238)
XLA Ops:
  0.7 163.6 %step.1 = (bf16[2,128,1024]{2,1,0:T(8,128)(2,1)}, f32[2,128,1024]{2,1,0:T(8,128)}, f32[8,3072]{1,0:T(8,128)}, f32[8,1024]{1,0:T(8,128)}, f32[8,4608]{1,0:T(8,128...) custom-call(f32[8,3072]{1,0:T(8,128)} %refs_2_.3, f32[8,1024]{1,0:T(8,128)} %refs_3_.3, ...), custom_call_target="tpu_custom_call" | custom-call | tf_op jit(solution)/shard_map/step/pallas_call | solution.py:1162
  164.3 5.0 %adamw.1 = (f32[2,8]{1,0:T(2,128)}, f32[3,8]{1,0:T(4,128)}, f32[8,3072]{1,0:T(8,128)}, f32[8,1024]{1,0:T(8,128)}, f32[8,4608]{1,0:T(8,128)}, /*index=5*/f32[8,46...) custom-call(f32[2,8]{1,0:T(2,128)} %refs_0_.3, ...), custom_call_target="tpu_custom_call" | custom-call | tf_op jit(solution)/shard_map/adamw/pallas_call | solution.py:1239
